TPU v7x, 32 devices: a whole 2x2x4 slice. The times are simulated.
32 devices in a mesh: groups: 2 (over y), space: 4 (over z), tangent: 4 (over x, core).
Axes of the slice: x: 2, y: 2, z: 4, core: 2. Of those that a mesh axis runs over, the one named last changes fastest.
Arguments:
- positions: float32 [16, 2, 128], P(('groups', 'space')), parts along dimension 0, may hold values from 0.45 to 15.55, as said below
- momenta: float32 [16, 2, 128], P(('groups', 'space')), parts along dimension 0, may hold values from -4 to 4
- cell_count: int32 [16], P(('groups', 'space')), parts along dimension 0, may hold values from 64 to 128, as said below
- tangent: float32 [16, 4, 128, 1024], P(('groups', 'space'), None, None, 'tangent'), parts along dimension 0, may hold values from -6 to 6
Outputs:
- phase: float32 [16, 4, 128], P(('groups', 'space')), parts along dimension 0
- new_tangent: float32 [16, 4, 128, 1024], P(('groups', 'space'), None, None, 'tangent'), parts along dimension 0
- stretch: float32 [2048], P(('groups', 'tangent')), parts along dimension 0
There are 2 independent parts, one for each index of `groups`. A program takes and returns all parts, laid end to end along the dimension named above; each array names one. Nothing has to cross between parts.
Inputs may be any that keep to these rules, and one draw needn't show every extreme that they name: Slots 0 to cell_count - 1 of a cell hold particles, the others are padding; some cell holds 128 particles in every draw. `positions`: every slot of a cell, padding too, lies within 0.05 in each coordinate of its own point of the lattice (m + 0.5, n + 0.5), m from 0 to 7, n from 0 to 15; no two slots of a cell share a lattice point.
All inputs are finite; a program needn't handle non-finite values.
Results may differ from a plain program's by a relative error of at most 0.006.
Values may be sent and summed in bfloat16 or wider, within the bound.
No kernel may reach another device: no remote copies, remote signals or barrier semaphores. Data moves between devices by JAX's collectives and lax.ppermute only.
A program may use at most 128 MiB of HBM per device.

v0:
```python
import jax
import jax.numpy as jnp
from jax import lax
from jax.experimental import pallas as pl
from jax.experimental.pallas import tpu as pltpu
from jax.sharding import PartitionSpec as P

STEPS = 2


DT = 0.005
CUT2 = 2.0 ** (1.0 / 3.0)
WIDE, TALL = 8, 16


BLOCK = 128
TILE = 8
BF16 = jnp.bfloat16
F32 = jnp.float32


def matmul(a, b, dims):
    return lax.dot_general(a, b, (dims, ((), ())), preferred_element_type=F32)


def two_parts(a):
    high = a.astype(BF16)
    return high, (a - high.astype(F32)).astype(BF16)


def three_pass(a, b, dims):
    a_high, a_low = two_parts(a)
    b_high, b_low = two_parts(b)
    return matmul(a_high, b_high, dims) + (matmul(a_high, b_low, dims) + matmul(a_low, b_high, dims))


def spread(row, sublane):
    return jnp.broadcast_to(row[sublane : sublane + 1, :], row.shape)


def factor_block(tiles):
    shape = tiles[0].shape
    sub = lax.broadcasted_iota(jnp.int32, shape, 0)
    lane = lax.broadcasted_iota(jnp.int32, shape, 1)
    tiles, rows_out, pivots = list(tiles), [], []
    for j, tile in enumerate(tiles):
        first = TILE * j
        cols = [jnp.broadcast_to(tile[:, first + k : first + k + 1], shape) for k in range(TILE)]
        inverse, ratio, rows = [], {}, []
        pivot = jnp.zeros(shape, F32)
        for k in range(TILE):
            top = spread(cols[k], k)
            pivot = jnp.where(sub == k, top, pivot)
            inverse.append(1.0 / top)
            for m in range(k + 1, TILE):
                ratio[k, m] = spread(cols[m], k) * inverse[k]
                cols[m] = cols[m] - cols[k] * ratio[k, m]
            rows.append(spread(tile, k) + jnp.where(lane == first + k, 1.0, 0.0))
            tile = tile - jnp.where(sub > k, cols[k] * inverse[k], 0.0) * rows[k]
        for i in range(j + 1, len(tiles)):
            cols = [jnp.broadcast_to(tiles[i][:, first + k : first + k + 1], shape) for k in range(TILE)]
            below = tiles[i]
            for k in range(TILE):
                for m in range(k + 1, TILE):
                    cols[m] = cols[m] - cols[k] * ratio[k, m]
                below = below - (cols[k] * inverse[k]) * rows[k]
            tiles[i] = below
        unit = jnp.where(lane < sub + first, tile, jnp.where(lane == sub + first, 1.0, 0.0))
        rows_out.append(unit * lax.rsqrt(pivot))
        pivots.append(pivot)
    return rows_out, pivots


def eliminate(total, work, pivots, small):
    def one_block(step, carry):
        top = pl.multiple_of(step * BLOCK, BLOCK)
        own = pl.ds(top, BLOCK)
        tiles = [work[pl.ds(top + TILE * i, TILE), own] for i in range(BLOCK // TILE)]
        rows_out, pivot_tiles = factor_block(tiles)
        for i in range(BLOCK // TILE):
            pivots[pl.ds(top + TILE * i, TILE), :] = pivot_tiles[i]
            small[TILE * i : TILE * (i + 1), :] = rows_out[i]
        inverse = small[...]

        def scale(col, carry):
            cols = pl.ds(pl.multiple_of(col * BLOCK, BLOCK), BLOCK)
            work[own, cols] = three_pass(inverse, work[own, cols], ((1,), (0,)))
            return carry

        lax.fori_loop(0, total, scale, 0)
        work[own, own] = inverse

        def trail(row, carry):
            rows = pl.ds(pl.multiple_of(row * BLOCK, BLOCK), BLOCK)
            work[rows, own] = jnp.zeros((BLOCK, BLOCK), F32)
            work[rows, :] = work[rows, :] - three_pass(work[own, rows].T, work[own, :], ((1,), (0,)))
            return carry

        lax.fori_loop(step + 1, total, trail, 0)
        return carry

    lax.fori_loop(0, total, one_block, 0)


def gram_kernel(shards, pieces, bc, x_refs, out_refs, part):
    me = lax.axis_index("tangent")
    here = lax.axis_index("space")
    half = bc // 2
    own = x_refs[0][...]
    part[0:bc, :] = matmul(own, own, ((0,), (0,)))
    for k in range(1, shards):
        rows = slice(bc + (k - 1) * half, bc + k * half)
        lower = me < (me ^ k)

        @pl.when(lower)
        def _():
            part[rows, :] = matmul(x_refs[0][:, 0:half], x_refs[k][...], ((0,), (0,)))

        @pl.when(jnp.logical_not(lower))
        def _():
            part[rows, :] = matmul(x_refs[k][:, half:bc], x_refs[0][...], ((0,), (0,)))

    size = part.shape[0] // pieces
    for k in range(pieces):
        start = pl.multiple_of(lax.rem(here + k, pieces) * size, 16)
        out_refs[k][...] = part[pl.ds(start, size), :]


def sum_kernel(in_refs, out_ref):
    total = in_refs[0][...]
    for ref in in_refs[1:]:
        total = total + ref[...]
    out_ref[...] = total


def solve_kernel(shards, pieces, bc, scale, g_refs, x_refs, out_ref, log_ref, work, pivots, small, part):
    me = lax.axis_index("tangent")
    here = lax.axis_index("space")
    half = bc // 2
    size = part.shape[0] // pieces
    for k in range(shards):
        peer = me ^ k
        for j in range(pieces):
            start = pl.multiple_of(lax.rem(here + pieces - j, pieces) * size, 16)
            part[pl.ds(start, size), :] = g_refs[k][j] * scale
        cols = pl.ds(pl.multiple_of(peer * bc, BLOCK), bc)
        work[cols, cols] = part[0:bc, :]
        for j in range(1, shards):
            other = peer ^ j
            low, high = jnp.minimum(peer, other), jnp.maximum(peer, other)
            top = pl.multiple_of(low * bc + jnp.where(peer == high, half, 0), half)
            work[pl.ds(top, half), pl.ds(pl.multiple_of(high * bc, BLOCK), bc)] = part[
                bc + (j - 1) * half : bc + j * half, :
            ]
    eliminate(shards * bc // BLOCK, work, pivots, small)
    mine = pl.ds(pl.multiple_of(me * bc, BLOCK), bc)
    row_block = lax.broadcasted_iota(jnp.int32, (bc, bc), 0) // BLOCK
    col_block = lax.broadcasted_iota(jnp.int32, (bc, bc), 1) // BLOCK

    def times(x_ref, factor):
        high, low = two_parts(factor)
        return matmul(x_ref[...], high, ((1,), (1,))) + matmul(x_ref[...], low, ((1,), (1,)))

    out_ref[...] = times(x_refs[0], jnp.where(row_block >= col_block, work[mine, mine], 0.0))
    for k in range(1, shards):
        peer = me ^ k

        @pl.when(peer < me)
        def _():
            cols = pl.ds(pl.multiple_of(peer * bc, BLOCK), bc)
            out_ref[...] += times(x_refs[k], work[mine, cols])

    eye = lax.broadcasted_iota(jnp.int32, (BLOCK, BLOCK), 0) == lax.broadcasted_iota(jnp.int32, (BLOCK, BLOCK), 1)
    for a in range(bc // BLOCK):
        block = pivots[pl.ds(pl.multiple_of(me * bc + a * BLOCK, BLOCK), BLOCK), :]
        log_ref[:, a * BLOCK : (a + 1) * BLOCK] = 0.5 * jnp.log(
            jnp.sum(jnp.where(eye, block, 0.0), axis=0, keepdims=True)
        )


def call(kernel, counts, out_shapes, scratch, operands):
    def unpacked(*refs):
        groups, at = [], 0
        for count in counts:
            groups.append(refs[at : at + count])
            at += count
        kernel(*groups, *refs[at:])

    return pl.pallas_call(
        unpacked,
        out_shape=out_shapes,
        scratch_shapes=scratch,
        compiler_params=pltpu.CompilerParams(vmem_limit_bytes=48 * 1024 * 1024),
    )(*operands)


def flip(array, axis, bit):
    return lax.ppermute(array, axis, [(i, i ^ bit) for i in range(lax.axis_size(axis))])


def orthonormalize(x):
    shards, pieces = lax.axis_size("tangent"), lax.axis_size("space")
    rows, bc = x.shape
    blocks = {0: x}
    bit = shards // 2
    while bit:
        blocks.update({k ^ bit: flip(v, "tangent", bit) for k, v in list(blocks.items())})
        bit //= 2
    blocks = [blocks[k] for k in range(shards)]
    held = bc + (shards - 1) * (bc // 2)
    direct = pieces <= 8
    cuts = pieces if direct else 1
    size = held // cuts
    piece = jax.ShapeDtypeStruct((size, bc), F32)

    def gram(*refs):
        gram_kernel(shards, cuts, bc, *refs)

    parts = call(
        gram, (shards, cuts), (piece,) * cuts, [pltpu.VMEM((held, bc), F32)], blocks
    )
    if direct:
        arrived = [parts[0]]
        for k in range(1, pieces):
            arrived.append(lax.ppermute(parts[k], "space", [(i, (i + k) % pieces) for i in range(pieces)]))
        total = call(lambda a, out: sum_kernel(a, out), (pieces,), piece, [], arrived)
        around = [total]
        for k in range(1, pieces):
            around.append(lax.ppermute(total, "space", [(i, (i + k) % pieces) for i in range(pieces)]))
        total = jnp.stack(around)
    else:
        total = lax.psum(parts[0], "space")[None]
    totals = {0: total}
    bit = shards // 2
    while bit:
        totals.update({k ^ bit: flip(v, "tangent", bit) for k, v in list(totals.items())})
        bit //= 2
    totals = [totals[k] for k in range(shards)]
    scale = 1.0 / (float(rows) * pieces)

    def solve(g_refs, x_refs, *refs):
        solve_kernel(shards, cuts, bc, scale, g_refs, x_refs, *refs)

    full = shards * bc
    out, logs = call(
        solve,
        (shards, shards),
        (jax.ShapeDtypeStruct((rows, bc), F32), jax.ShapeDtypeStruct((1, bc), F32)),
        [
            pltpu.VMEM((full, full), F32),
            pltpu.VMEM((full, BLOCK), F32),
            pltpu.VMEM((BLOCK, BLOCK), F32),
            pltpu.VMEM((held, bc), F32),
        ],
        totals + blocks,
    )
    return out, logs[0]


def lattice_rows(raw_ref, first, count):
    cells = raw_ref.shape[0]
    high = cells * TALL
    sites = [
        raw_ref[c, 0:1, :].astype(jnp.int32) * high + raw_ref[c, 1:2, :].astype(jnp.int32) + c * TALL
        for c in range(cells)
    ]
    site = jnp.concatenate(sites, axis=1)
    rows = lax.broadcasted_iota(jnp.int32, (count, site.shape[1]), 0) + first
    return jnp.where(rows == site, 1.0, 0.0).astype(BF16)


def three_parts(a):
    high, rest = a.astype(BF16), None
    rest = a - high.astype(F32)
    mid = rest.astype(BF16)
    return high, mid, (rest - mid.astype(F32)).astype(BF16)


def sort_kernel(raw_ref, count_ref, tangent_ref, state_ref, left_ref, right_ref):
    cells, comps, slots, bc = tangent_ref.shape
    high = cells * TALL
    place = lattice_rows(raw_ref, 0, high * WIDE)
    slot = lax.broadcasted_iota(jnp.int32, (slots, bc), 0)
    for comp in range(comps):
        rows = [jnp.where(slot < count_ref[c], tangent_ref[c, comp], 0.0) for c in range(cells)]
        top, low = two_parts(jnp.concatenate(rows, axis=0))
        moved = matmul(place, top, ((1,), (0,))) + matmul(place, low, ((1,), (0,)))
        state_ref[comp] = moved.reshape(WIDE, high, bc)
        near = moved.astype(BF16).reshape(WIDE, high, bc)
        if comp < 2:
            left_ref[3 * comp : 3 * comp + 3] = near[0:3]
            right_ref[3 * comp : 3 * comp + 3] = near[WIDE - 3 :]
        else:
            at = 6 + 2 * (comp - 2)
            left_ref[at : at + 2] = near[0:2]
            right_ref[at : at + 2] = near[WIDE - 2 :]


def bond(far_x, far_y, own_x, own_y, both, shift_x, shift_y):
    dx = shift_x + far_x - own_x
    dy = shift_y + far_y - own_y
    dist2 = dx * dx + dy * dy
    within = jnp.logical_and(dist2 < CUT2, both > 0.5)
    weight = jnp.where(within, 1.0, 0.0)
    safe = jnp.where(within, dist2, CUT2)
    inverse = 1.0 / safe
    inv_three = inverse * inverse * inverse
    inv_six = inv_three * inv_three
    energy = 4.0 * (inv_six - inv_three) + 1.0
    energy_1 = 4.0 * (3.0 * inv_three - 6.0 * inv_six) * inverse
    energy_2 = 4.0 * (42.0 * inv_six - 12.0 * inv_three) * inverse * inverse
    taper = 1.0 - safe * (1.0 / CUT2)
    switch = taper * taper
    switch_1 = taper * (-2.0 / CUT2)
    switch_2 = 2.0 / (CUT2 * CUT2)
    twice_1 = (energy_1 * switch + energy * switch_1) * weight * 2.0
    four_2 = (energy_2 * switch + 2.0 * energy_1 * switch_1 + energy * switch_2) * weight * 4.0
    k_xx = twice_1 + four_2 * dx * dx
    k_xy = four_2 * dx * dy
    k_yy = twice_1 + four_2 * dy * dy
    return twice_1 * dx, twice_1 * dy, (k_xx, k_xy, k_yy)


def up(a):
    return pltpu.roll(a, a.shape[0] - 1, 0)


def down(a):
    return pltpu.roll(a, 1, 0)


KICKS = tuple((0.5 if step in (0, STEPS) else 1.0) * DT for step in range(STEPS + 1))


def path_kernel(raw_ref, low_ref, high_ref, phase_ref, k_ref, lat):
    cells, _, slots = raw_ref.shape
    tall = cells * TALL
    halo = STEPS + 1
    columns = WIDE + 2 * halo
    own = lattice_rows(raw_ref, 0, WIDE * tall)
    sides = (
        (low_ref, lattice_rows(low_ref, (WIDE - halo) * tall, halo * tall), 0, halo),
        (raw_ref, own, halo, WIDE),
        (high_ref, lattice_rows(high_ref, 0, halo * tall), halo + WIDE, halo),
    )
    for ref, place, first, width in sides:
        for item in range(5):
            row = jnp.concatenate([ref[c, item : item + 1, :] for c in range(cells)], axis=1)
            wide = jnp.broadcast_to(row, (BLOCK, row.shape[1]))
            parts = three_parts(wide) if item < 4 else (wide.astype(BF16),)
            value = sum(matmul(place, part, ((1,), (1,))) for part in parts)
            lat[item, first : first + width] = value.reshape(width, tall, BLOCK)
    site = lax.broadcasted_iota(jnp.int32, (tall, BLOCK), 0)
    shift_y = jnp.where(lax.rem(site, TALL) == TALL - 1, float(TALL), 0.0)
    zero = jnp.zeros((tall, BLOCK), F32)
    for step, kick in enumerate(KICKS):
        move = DT if step < STEPS else 0.0

        def column(c, carry):
            x, y, alive, pull_x, pull_y = carry
            far_x, far_y, far_alive = lat[0, c + 1], lat[1, c + 1], lat[4, c + 1]
            crossing = jnp.logical_or(c == halo - 1, c == halo + WIDE - 1)
            shift_x = jnp.where(crossing, float(WIDE), 0.0)
            side_x, side_y, k_side = bond(far_x, far_y, x, y, alive * far_alive, shift_x, 0.0)
            over_x, over_y, k_over = bond(up(x), up(y), x, y, alive * up(alive), 0.0, shift_y)
            for a in range(3):
                k_ref[step, a, c] = k_side[a].astype(BF16)
                k_ref[step, 3 + a, c] = k_over[a].astype(BF16)
            speed_x = lat[2, c] + kick * (side_x - pull_x + over_x - down(over_x))
            speed_y = lat[3, c] + kick * (side_y - pull_y + over_y - down(over_y))
            lat[2, c], lat[3, c] = speed_x, speed_y
            if move:
                lat[0, c], lat[1, c] = x + move * speed_x, y + move * speed_y
            return far_x, far_y, far_alive, side_x, side_y

        start = (lat[0, step], lat[1, step], lat[4, step], zero, zero)
        lax.fori_loop(step, columns - 1 - step, column, start)
    for item in range(4):
        value = lat[item, halo : halo + WIDE, :, 0:TILE].reshape(WIDE * tall, TILE)
        back = sum(matmul(part, own, ((0,), (0,))) for part in three_parts(value))
        for c in range(cells):
            phase_ref[c, item : item + 1, :] = back[0:1, c * slots : (c + 1) * slots]


def tangent_kernel(raw_ref, k_ref, state_ref, low_ref, high_ref, x_ref, wide):
    cells, comps, slots, bc = x_ref.shape
    tall = cells * TALL
    halo = STEPS + 1
    columns = WIDE + 2 * halo
    for comp in range(comps):
        wide[comp, halo : halo + WIDE] = state_ref[comp]
        if comp < 2:
            wide[comp, 0:halo] = low_ref[3 * comp : 3 * comp + 3].astype(F32)
            wide[comp, halo + WIDE :] = high_ref[3 * comp : 3 * comp + 3].astype(F32)
        else:
            at = 6 + 2 * (comp - 2)
            wide[comp, 1:halo] = low_ref[at : at + 2].astype(F32)
            wide[comp, halo + WIDE : columns - 1] = high_ref[at : at + 2].astype(F32)
    zero = jnp.zeros((tall, bc), F32)

    def rounded(comp, c):
        return wide[comp, c].astype(BF16).astype(F32)

    def stretched(step, a, c):
        k = k_ref[step, a, c].astype(F32)
        return jnp.concatenate([k] * (bc // BLOCK), axis=1)

    for step, kick in enumerate(KICKS):
        move = DT if step < STEPS else 0.0

        def push(c, k0, e_x, e_y):
            k_xx, k_xy, k_yy = [stretched(step, k0 + a, c) for a in range(3)]
            return k_xx * e_x + k_xy * e_y, k_xy * e_x + k_yy * e_y

        def column(c, carry):
            x, y, pull_x, pull_y = carry
            far_x, far_y = rounded(0, c + 1), rounded(1, c + 1)
            side_x, side_y = push(c, 0, far_x - x, far_y - y)
            over_x, over_y = push(c, 3, up(x) - x, up(y) - y)
            speed_x = wide[2, c] + kick * (side_x - pull_x + over_x - down(over_x))
            speed_y = wide[3, c] + kick * (side_y - pull_y + over_y - down(over_y))
            wide[2, c], wide[3, c] = speed_x, speed_y
            if move:
                wide[0, c] = wide[0, c] + move * speed_x
                wide[1, c] = wide[1, c] + move * speed_y
            return far_x, far_y, side_x, side_y

        x, y = rounded(0, step), rounded(1, step)
        first = push(step, 0, rounded(0, step + 1) - x, rounded(1, step + 1) - y)
        start = (rounded(0, step + 1), rounded(1, step + 1)) + first
        lax.fori_loop(step + 1, columns - 1 - step, column, start)
    place = lattice_rows(raw_ref, 0, WIDE * tall)
    for comp in range(comps):
        value = wide[comp, halo : halo + WIDE].reshape(WIDE * tall, bc).astype(BF16)
        back = matmul(place, value, ((0,), (0,))).astype(BF16)
        for c in range(cells):
            x_ref[c, comp] = back[c * slots : (c + 1) * slots]


def dynamics(positions, momenta, cell_count, tangent):
    cells, comps, slots, bc = tangent.shape
    tall = cells * TALL
    columns = WIDE + 2 * (STEPS + 1)
    occupied = (lax.broadcasted_iota(jnp.int32, (cells, 1, slots), 2) < cell_count[:, None, None]).astype(F32)
    raw = jnp.concatenate([positions, momenta, occupied], axis=1)
    count = lax.axis_size("space")
    forward = [(i, (i + 1) % count) for i in range(count)]
    backward = [(b, a) for a, b in forward]
    raw_low, raw_high = lax.ppermute(raw, "space", forward), lax.ppermute(raw, "space", backward)
    halo = jax.ShapeDtypeStruct((10, tall, bc), BF16)
    vmem = pl.BlockSpec(memory_space=pltpu.VMEM)
    params = pltpu.CompilerParams(vmem_limit_bytes=48 * 1024 * 1024)
    state, left, right = pl.pallas_call(
        sort_kernel,
        out_shape=(jax.ShapeDtypeStruct((comps, WIDE, tall, bc), F32), halo, halo),
        in_specs=[vmem, pl.BlockSpec(memory_space=pltpu.SMEM), vmem],
        compiler_params=params,
    )(raw, cell_count, tangent)
    low, high = lax.ppermute(right, "space", forward), lax.ppermute(left, "space", backward)
    phase, k = pl.pallas_call(
        path_kernel,
        out_shape=(
            jax.ShapeDtypeStruct((cells, 4, slots), F32),
            jax.ShapeDtypeStruct((STEPS + 1, 6, columns, tall, BLOCK), BF16),
        ),
        scratch_shapes=[pltpu.VMEM((5, columns, tall, BLOCK), F32)],
        compiler_params=params,
        cost_estimate=pl.CostEstimate(flops=4 * 10**9, bytes_accessed=4 * 10**6, transcendentals=0),
    )(raw, raw_low, raw_high)
    x = pl.pallas_call(
        tangent_kernel,
        out_shape=jax.ShapeDtypeStruct(tangent.shape, BF16),
        scratch_shapes=[pltpu.VMEM((comps, columns, tall, bc), F32)],
        compiler_params=params,
    )(raw, k, state, low, high)
    return phase, x


def body(positions, momenta, cell_count, tangent):
    phase, x = dynamics(positions, momenta, cell_count, tangent)
    out, stretch = orthonormalize(x.reshape(-1, x.shape[3]))
    return (phase, out.reshape(x.shape), stretch)


def solution(mesh):
    placed = (
        P(("groups", "space"), None, None),
        P(("groups", "space"), None, None),
        P(("groups", "space")),
        P(("groups", "space"), None, None, "tangent"),
    )
    return jax.shard_map(
        body,
        mesh=mesh,
        in_specs=placed,
        out_specs=(
            P(("groups", "space"), None, None),
            P(("groups", "space"), None, None, "tangent"),
            P(("groups", "tangent")),
        ),
        check_vma=False,
    )
```

profile of v0, /device:TPU:7, one launch (start us, length us, event | category | flops | bytes accessed | tf_op | source)
XLA Modules:
  0.0 148.2 jit_solution(490264689681604085)
XLA Ops:
  0.6 0.7 compare_convert_fusion
  1.4 0.7 pad_maximum_fusion.1.raw_ref
  2.1 3.3 %collective-permute-start.1 = (f32[2,5,128]{2,1,0:T(8,128)S(1)}, f32[2,5,128]{2,1,0:T(8,128)S(1)}, u32[]{:S(2)}, u32[]{:S(2)}) collective-permute-start(f32[2,5,128]{2,1,0:T(8,128)S(1)} %pad_maximum_fusion.1.raw_ref), channel_id=1, source_target_pairs={{4,0},{8,4},{12,8},{0,12},{5,1},{9,5},{13,9},{1,13},{6,2},{10,6},{... | collective-permute-start | bytes 15368 | tf_op jit(solution)/shard_map/ppermute | solution.py:449
  5.4 0.0 collective-permute-start
  5.4 1.2 copy-done
  6.6 0.7 copy-done.1
  7.3 1.1 shard_map.68
  8.4 0.1 collective-permute-start.2
  8.4 3.3 %collective-permute-start.3 = (bf16[10,32,256]{2,1,0:T(8,128)(2,1)S(1)}, bf16[10,32,256]{2,1,0:T(8,128)(2,1)S(1)}, u32[]{:S(2)}, u32[]{:S(2)}) collective-permute-start(bf16[10,32,256]{2,1,0:T(8,128)(2,1)S(1)} %get-tuple-element.18), channel_id=1, source_target_pairs={{4,0},{8,4},{12,8},{0,12},{5,1},{9,5},{13,9},{1,13},{6,2},{10,6},{... | collective-permute-start | bytes 491528 | tf_op jit(solution)/shard_map/ppermute | solution.py:459
  11.7 4.8 %shard_map.67 = (f32[2,4,128]{2,1,0:T(4,128)}, bf16[3,6,14,32,128]{4,3,2,1,0:T(8,128)(2,1)S(1)}) custom-call(f32[2,5,128]{2,1,0:T(8,128)S(1)} %pad_maximum_fusion.1.raw_ref, f32[2,5,128]{2,1,0:T(8,128)S(1)} %collective-permute-done.low_ref, f32[2,5,128]{2,1,0:T(8,128)S(1)} %collective-permute-done.1.high_ref), custom_call_target="tpu_custom_call" | custom-call | flops 4000000000 | bytes 4000000 | tf_op jit(solution)/shard_map/pallas_call | solution.py:460
  16.6 2.2 %shard_map.69 = bf16[2,4,128,256]{3,2,1,0:T(8,128)(2,1)S(1)} custom-call(f32[2,5,128]{2,1,0:T(8,128)S(1)} %pad_maximum_fusion.1.raw_ref, bf16[3,6,14,32,128]{4,3,2,1,0:T(8,128)(2,1)S(1)} %get-tuple-element.15.k_ref, f32[4,8,32,256]{3,2,1,0:T(8,128)S(1)} %get-tuple-element.16.state_ref, bf16[10,32,256]{2,1,0:T(8,128)(2,1)S(1)} %collective-permute-done.2.low_ref, ...), custom_call_target="tpu_custom_call" | custom-call | tf_op jit(solution)/shard_map/pallas_call | solution.py:470
  18.7 0.3 collective-permute-start.5
  19.1 2.4 %collective-permute-start.4 = (bf16[1024,256]{1,0:T(8,128)(2,1)S(1)}, bf16[1024,256]{1,0:T(8,128)(2,1)S(1)}, u32[]{:S(2)}, u32[]{:S(2)}) collective-permute-start(bf16[1024,256]{1,0:T(8,128)(2,1)S(1)} %bitcast.8), channel_id=1, source_target_pairs={{0,1},{1,0},{2,3},{3,2},{4,5},{5,4},{6,7},{7,6},{8,9},{9,8},{10,11... | collective-permute-start | bytes 1572872 | tf_op jit(solution)/shard_map/ppermute | solution.py:198
  21.5 8.6 %collective-permute-done.5.refs_2_.refs_6_ = bf16[1024,256]{1,0:T(8,128)(2,1)S(1)} collective-permute-done((bf16[1024,256]{1,0:T(8,128)(2,1)S(1)}, bf16[1024,256]{1,0:T(8,128)(2,1)S(1)}, u32[]{:S(2)}, u32[]{:S(2)}) %collective-permute-start.5) | collective-permute-done | bytes 524320 | tf_op jit(solution)/shard_map/ppermute | solution.py:198
  30.1 3.0 %collective-permute-start.6 = (bf16[1024,256]{1,0:T(8,128)(2,1)S(1)}, bf16[1024,256]{1,0:T(8,128)(2,1)S(1)}, u32[]{:S(2)}, u32[]{:S(2)}) collective-permute-start(bf16[1024,256]{1,0:T(8,128)(2,1)S(1)} %collective-permute-done.5.refs_2_.refs_6_), channel_id=1, source_target_pairs={{0,1},{1,0},{2,3},{3,2},{4,5},{5,4},{6,7},{7,6},{8,9},{9,8},{10,11... | collective-permute-start | bytes 1572872 | tf_op jit(solution)/shard_map/ppermute | solution.py:198
  33.1 0.0 collective-permute-done.4.refs_1_.refs_5_
  33.1 1.5 %collective-permute-done.6.refs_3_.refs_7_ = bf16[1024,256]{1,0:T(8,128)(2,1)S(1)} collective-permute-done((bf16[1024,256]{1,0:T(8,128)(2,1)S(1)}, bf16[1024,256]{1,0:T(8,128)(2,1)S(1)}, u32[]{:S(2)}, u32[]{:S(2)}) %collective-permute-start.6) | collective-permute-done | bytes 524320 | tf_op jit(solution)/shard_map/ppermute | solution.py:198
  34.7 1.2 shard_map.70
  35.9 3.6 %collective-permute-start.7 = (f32[160,256]{1,0:T(8,128)S(1)}, f32[160,256]{1,0:T(8,128)S(1)}, u32[]{:S(2)}, u32[]{:S(2)}) collective-permute-start(f32[160,256]{1,0:T(8,128)S(1)} %get-tuple-element.20), channel_id=1, source_target_pairs={{0,4},{4,8},{8,12},{12,0},{1,5},{5,9},{9,13},{13,1},{2,6},{6,10},{... | collective-permute-start | bytes 491528 | tf_op jit(solution)/shard_map/ppermute | solution.py:225
  39.5 2.2 %collective-permute-start.9 = (f32[160,256]{1,0:T(8,128)S(1)}, f32[160,256]{1,0:T(8,128)S(1)}, u32[]{:S(2)}, u32[]{:S(2)}) collective-permute-start(f32[160,256]{1,0:T(8,128)S(1)} %get-tuple-element.22), channel_id=1, source_target_pairs={{0,12},{4,0},{8,4},{12,8},{1,13},{5,1},{9,5},{13,9},{2,14},{6,2},{... | collective-permute-start | bytes 491528 | tf_op jit(solution)/shard_map/ppermute | solution.py:225
  41.7 1.5 %collective-permute-done.7.refs_1_ = f32[160,256]{1,0:T(8,128)S(1)} collective-permute-done((f32[160,256]{1,0:T(8,128)S(1)}, f32[160,256]{1,0:T(8,128)S(1)}, u32[]{:S(2)}, u32[]{:S(2)}) %collective-permute-start.7) | collective-permute-done | bytes 163872 | tf_op jit(solution)/shard_map/ppermute | solution.py:225
  43.2 7.7 %collective-permute-done.8.refs_2_ = f32[160,256]{1,0:T(8,128)S(1)} collective-permute-done((f32[160,256]{1,0:T(8,128)S(1)}, f32[160,256]{1,0:T(8,128)S(1)}, u32[]{:S(2)}, u32[]{:S(2)}) %collective-permute-start.8) | collective-permute-done | bytes 163872 | tf_op jit(solution)/shard_map/ppermute | solution.py:225
  50.9 5.6 %collective-permute-start.12 = (f32[160,256]{1,0:T(8,128)S(1)}, f32[160,256]{1,0:T(8,128)S(1)}, u32[]{:S(2)}, u32[]{:S(2)}) collective-permute-start(f32[160,256]{1,0:T(8,128)S(1)} %shard_map.71), channel_id=1, source_target_pairs={{0,12},{4,0},{8,4},{12,8},{1,13},{5,1},{9,5},{13,9},{2,14},{6,2},{... | collective-permute-start | bytes 491528 | tf_op jit(solution)/shard_map/ppermute | solution.py:229
  56.5 0.4 collective-permute-start.10
  56.9 2.4 %collective-permute-done.12 = f32[160,256]{1,0:T(8,128)S(1)} collective-permute-done((f32[160,256]{1,0:T(8,128)S(1)}, f32[160,256]{1,0:T(8,128)S(1)}, u32[]{:S(2)}, u32[]{:S(2)}) %collective-permute-start.12) | collective-permute-done | bytes 163872 | tf_op jit(solution)/shard_map/ppermute | solution.py:229
  59.3 11.5 %collective-permute-done.11 = f32[160,256]{1,0:T(8,128)S(1)} collective-permute-done((f32[160,256]{1,0:T(8,128)S(1)}, f32[160,256]{1,0:T(8,128)S(1)}, u32[]{:S(2)}, u32[]{:S(2)}) %collective-permute-start.11) | collective-permute-done | bytes 163872 | tf_op jit(solution)/shard_map/ppermute | solution.py:229
  70.8 0.3 collective-permute-start.14
  71.1 1.2 collective-permute-start.13
  72.3 13.9 %collective-permute-done.14.refs_2_ = f32[4,160,256]{2,1,0:T(8,128)S(1)} collective-permute-done((f32[4,160,256]{2,1,0:T(8,128)S(1)}, f32[4,160,256]{2,1,0:T(8,128)S(1)}, u32[]{:S(2)}, u32[]{:S(2)}) %collective-permute-start.14) | collective-permute-done | bytes 655392 | tf_op jit(solution)/shard_map/ppermute | solution.py:198
  86.2 1.8 %collective-permute-start.15 = (f32[4,160,256]{2,1,0:T(8,128)S(1)}, f32[4,160,256]{2,1,0:T(8,128)S(1)}, u32[]{:S(2)}, u32[]{:S(2)}) collective-permute-start(f32[4,160,256]{2,1,0:T(8,128)S(1)} %collective-permute-done.14.refs_2_), channel_id=1, source_target_pairs={{0,1},{1,0},{2,3},{3,2},{4,5},{5,4},{6,7},{7,6},{8,9},{9,8},{10,11... | collective-permute-start | bytes 1966088 | tf_op jit(solution)/shard_map/ppermute | solution.py:198
  88.0 1.7 %collective-permute-done.15.refs_3_ = f32[4,160,256]{2,1,0:T(8,128)S(1)} collective-permute-done((f32[4,160,256]{2,1,0:T(8,128)S(1)}, f32[4,160,256]{2,1,0:T(8,128)S(1)}, u32[]{:S(2)}, u32[]{:S(2)}) %collective-permute-start.15) | collective-permute-done | bytes 655392 | tf_op jit(solution)/shard_map/ppermute | solution.py:198
  89.7 58.5 %shard_map.72 = (f32[1024,256]{1,0:T(8,128)}, f32[1,256]{1,0:T(1,128)}) custom-call(f32[4,160,256]{2,1,0:T(8,128)S(1)} %pad_maximum_fusion.refs_0_, f32[4,160,256]{2,1,0:T(8,128)S(1)} %collective-permute-done.13.refs_1_, f32[4,160,256]{2,1,0:T(8,128)S(1)} %collective-permute-done.14.refs_2_, f32[4,160,256]{2,1,0:T(8,128)S(1)} %collective-permute-done.15.refs_3_, ...), custom_call_target="tpu_custom_call" | custom-call | tf_op jit(solution)/shard_map/pallas_call | solution.py:189
  (13 shorter events, 0.1 us)
Async XLA Ops:
  2.1 9.7 %collective-permute-start.1 = (f32[2,5,128]{2,1,0:T(8,128)S(1)}, f32[2,5,128]{2,1,0:T(8,128)S(1)}, u32[]{:S(2)}, u32[]{:S(2)}) collective-permute-start(f32[2,5,128]{2,1,0:T(8,128)S(1)} %pad_maximum_fusion.1.raw_ref), channel_id=1, source_target_pairs={{4,0},{8,4},{12,8},{0,12},{5,1},{9,5},{13,9},{1,13},{6,2},{10,6},{... | collective-permute-start | bytes 15368 | tf_op jit(solution)/shard_map/ppermute | solution.py:449
  5.4 6.4 %collective-permute-start = (f32[2,5,128]{2,1,0:T(8,128)S(1)}, f32[2,5,128]{2,1,0:T(8,128)S(1)}, u32[]{:S(2)}, u32[]{:S(2)}) collective-permute-start(f32[2,5,128]{2,1,0:T(8,128)S(1)} %pad_maximum_fusion.1.raw_ref), channel_id=1, source_target_pairs={{0,4},{4,8},{8,12},{12,0},{1,5},{5,9},{9,13},{13,1},{2,6},{6,10},{... | collective-permute-start | bytes 15368 | tf_op jit(solution)/shard_map/ppermute | solution.py:449
  5.4 1.2 copy-start
  6.6 0.7 copy-start.1
  8.4 8.2 %collective-permute-start.2 = (bf16[10,32,256]{2,1,0:T(8,128)(2,1)S(1)}, bf16[10,32,256]{2,1,0:T(8,128)(2,1)S(1)}, u32[]{:S(2)}, u32[]{:S(2)}) collective-permute-start(bf16[10,32,256]{2,1,0:T(8,128)(2,1)S(1)} %get-tuple-element.17), channel_id=1, source_target_pairs={{0,4},{4,8},{8,12},{12,0},{1,5},{5,9},{9,13},{13,1},{2,6},{6,10},{... | collective-permute-start | bytes 491528 | tf_op jit(solution)/shard_map/ppermute | solution.py:459
  8.4 8.1 %collective-permute-start.3 = (bf16[10,32,256]{2,1,0:T(8,128)(2,1)S(1)}, bf16[10,32,256]{2,1,0:T(8,128)(2,1)S(1)}, u32[]{:S(2)}, u32[]{:S(2)}) collective-permute-start(bf16[10,32,256]{2,1,0:T(8,128)(2,1)S(1)} %get-tuple-element.18), channel_id=1, source_target_pairs={{4,0},{8,4},{12,8},{0,12},{5,1},{9,5},{13,9},{1,13},{6,2},{10,6},{... | collective-permute-start | bytes 491528 | tf_op jit(solution)/shard_map/ppermute | solution.py:459
  18.7 11.4 %collective-permute-start.5 = (bf16[1024,256]{1,0:T(8,128)(2,1)S(1)}, bf16[1024,256]{1,0:T(8,128)(2,1)S(1)}, u32[]{:S(2)}, u32[]{:S(2)}) collective-permute-start(bf16[1024,256]{1,0:T(8,128)(2,1)S(1)} %bitcast.7), channel_id=1, source_target_pairs={{0,2},{1,3},{2,0},{3,1},{4,6},{5,7},{6,4},{7,5},{8,10},{9,11},{10,... | collective-permute-start | bytes 1572872 | tf_op jit(solution)/shard_map/ppermute | solution.py:198
  19.1 14.1 %collective-permute-start.4 = (bf16[1024,256]{1,0:T(8,128)(2,1)S(1)}, bf16[1024,256]{1,0:T(8,128)(2,1)S(1)}, u32[]{:S(2)}, u32[]{:S(2)}) collective-permute-start(bf16[1024,256]{1,0:T(8,128)(2,1)S(1)} %bitcast.8), channel_id=1, source_target_pairs={{0,1},{1,0},{2,3},{3,2},{4,5},{5,4},{6,7},{7,6},{8,9},{9,8},{10,11... | collective-permute-start | bytes 1572872 | tf_op jit(solution)/shard_map/ppermute | solution.py:198
  30.1 4.6 %collective-permute-start.6 = (bf16[1024,256]{1,0:T(8,128)(2,1)S(1)}, bf16[1024,256]{1,0:T(8,128)(2,1)S(1)}, u32[]{:S(2)}, u32[]{:S(2)}) collective-permute-start(bf16[1024,256]{1,0:T(8,128)(2,1)S(1)} %collective-permute-done.5.refs_2_.refs_6_), channel_id=1, source_target_pairs={{0,1},{1,0},{2,3},{3,2},{4,5},{5,4},{6,7},{7,6},{8,9},{9,8},{10,11... | collective-permute-start | bytes 1572872 | tf_op jit(solution)/shard_map/ppermute | solution.py:198
  35.9 7.3 %collective-permute-start.7 = (f32[160,256]{1,0:T(8,128)S(1)}, f32[160,256]{1,0:T(8,128)S(1)}, u32[]{:S(2)}, u32[]{:S(2)}) collective-permute-start(f32[160,256]{1,0:T(8,128)S(1)} %get-tuple-element.20), channel_id=1, source_target_pairs={{0,4},{4,8},{8,12},{12,0},{1,5},{5,9},{9,13},{13,1},{2,6},{6,10},{... | collective-permute-start | bytes 491528 | tf_op jit(solution)/shard_map/ppermute | solution.py:225
  39.5 11.4 %collective-permute-start.8 = (f32[160,256]{1,0:T(8,128)S(1)}, f32[160,256]{1,0:T(8,128)S(1)}, u32[]{:S(2)}, u32[]{:S(2)}) collective-permute-start(f32[160,256]{1,0:T(8,128)S(1)} %get-tuple-element.21), channel_id=1, source_target_pairs={{0,8},{4,12},{8,0},{12,4},{1,9},{5,13},{9,1},{13,5},{2,10},{6,14},... | collective-permute-start | bytes 491528 | tf_op jit(solution)/shard_map/ppermute | solution.py:225
  39.5 11.4 %collective-permute-start.9 = (f32[160,256]{1,0:T(8,128)S(1)}, f32[160,256]{1,0:T(8,128)S(1)}, u32[]{:S(2)}, u32[]{:S(2)}) collective-permute-start(f32[160,256]{1,0:T(8,128)S(1)} %get-tuple-element.22), channel_id=1, source_target_pairs={{0,12},{4,0},{8,4},{12,8},{1,13},{5,1},{9,5},{13,9},{2,14},{6,2},{... | collective-permute-start | bytes 491528 | tf_op jit(solution)/shard_map/ppermute | solution.py:225
  50.9 8.3 %collective-permute-start.12 = (f32[160,256]{1,0:T(8,128)S(1)}, f32[160,256]{1,0:T(8,128)S(1)}, u32[]{:S(2)}, u32[]{:S(2)}) collective-permute-start(f32[160,256]{1,0:T(8,128)S(1)} %shard_map.71), channel_id=1, source_target_pairs={{0,12},{4,0},{8,4},{12,8},{1,13},{5,1},{9,5},{13,9},{2,14},{6,2},{... | collective-permute-start | bytes 491528 | tf_op jit(solution)/shard_map/ppermute | solution.py:229
  56.5 14.2 %collective-permute-start.11 = (f32[160,256]{1,0:T(8,128)S(1)}, f32[160,256]{1,0:T(8,128)S(1)}, u32[]{:S(2)}, u32[]{:S(2)}) collective-permute-start(f32[160,256]{1,0:T(8,128)S(1)} %shard_map.71), channel_id=1, source_target_pairs={{0,8},{4,12},{8,0},{12,4},{1,9},{5,13},{9,1},{13,5},{2,10},{6,14},... | collective-permute-start | bytes 491528 | tf_op jit(solution)/shard_map/ppermute | solution.py:229
  56.5 14.2 %collective-permute-start.10 = (f32[160,256]{1,0:T(8,128)S(1)}, f32[160,256]{1,0:T(8,128)S(1)}, u32[]{:S(2)}, u32[]{:S(2)}) collective-permute-start(f32[160,256]{1,0:T(8,128)S(1)} %shard_map.71), channel_id=1, source_target_pairs={{0,4},{4,8},{8,12},{12,0},{1,5},{5,9},{9,13},{13,1},{2,6},{6,10},{... | collective-permute-start | bytes 491528 | tf_op jit(solution)/shard_map/ppermute | solution.py:229
  70.8 15.4 %collective-permute-start.14 = (f32[4,160,256]{2,1,0:T(8,128)S(1)}, f32[4,160,256]{2,1,0:T(8,128)S(1)}, u32[]{:S(2)}, u32[]{:S(2)}) collective-permute-start(f32[4,160,256]{2,1,0:T(8,128)S(1)} %pad_maximum_fusion.refs_0_), channel_id=1, source_target_pairs={{0,2},{1,3},{2,0},{3,1},{4,6},{5,7},{6,4},{7,5},{8,10},{9,11},{10,... | collective-permute-start | bytes 1966088 | tf_op jit(solution)/shard_map/ppermute | solution.py:198
  71.1 16.9 %collective-permute-start.13 = (f32[4,160,256]{2,1,0:T(8,128)S(1)}, f32[4,160,256]{2,1,0:T(8,128)S(1)}, u32[]{:S(2)}, u32[]{:S(2)}) collective-permute-start(f32[4,160,256]{2,1,0:T(8,128)S(1)} %pad_maximum_fusion.refs_0_), channel_id=1, source_target_pairs={{0,1},{1,0},{2,3},{3,2},{4,5},{5,4},{6,7},{7,6},{8,9},{9,8},{10,11... | collective-permute-start | bytes 1966088 | tf_op jit(solution)/shard_map/ppermute | solution.py:198
  86.2 3.6 %collective-permute-start.15 = (f32[4,160,256]{2,1,0:T(8,128)S(1)}, f32[4,160,256]{2,1,0:T(8,128)S(1)}, u32[]{:S(2)}, u32[]{:S(2)}) collective-permute-start(f32[4,160,256]{2,1,0:T(8,128)S(1)} %collective-permute-done.14.refs_2_), channel_id=1, source_target_pairs={{0,1},{1,0},{2,3},{3,2},{4,5},{5,4},{6,7},{7,6},{8,9},{9,8},{10,11... | collective-permute-start | bytes 1966088 | tf_op jit(solution)/shard_map/ppermute | solution.py:198
where the time goes:
time: 148 us
  Pallas kernels  67.8 us (46%)
  waiting for transfers between devices  48.8 us (33%)
  starting transfers between devices  27.6 us (19%)
  local copies, waits for them, and re-layouts  1.88 us (1%)
  other arithmetic  1.48 us (1%)
    pallas_call x3, Pallas kernels, call(): pl.pallas_call(unpacked, out_shape=out_shapes, scratch_shapes=scratch, co...  59.7 us
    ppermute x6, waiting for transfers between devices, flip(): lax.ppermute(array, axis, [(i, i ^ bit) for i in range(lax.axis_size(axis...  25.7 us
    ppermute x3, waiting for transfers between devices, orthonormalize(): lax.ppermute(total, 'space', [(i, (i + k) % pieces) for i in range(pieces)])  13.8 us
    ppermute x3, waiting for transfers between devices, orthonormalize(): lax.ppermute(parts[k], 'space', [(i, (i + k) % pieces) for i in range(pie...  9.21 us
    ppermute x6, starting transfers between devices, flip(): lax.ppermute(array, axis, [(i, i ^ bit) for i in range(lax.axis_size(axis...  9.13 us
    ppermute x3, starting transfers between devices, orthonormalize(): lax.ppermute(total, 'space', [(i, (i + k) % pieces) for i in range(pieces)])  5.94 us
    ppermute x3, starting transfers between devices, orthonormalize(): lax.ppermute(parts[k], 'space', [(i, (i + k) % pieces) for i in range(pie...  5.78 us
    pallas_call x1, Pallas kernels, dynamics(): pl.pallas_call(path_kernel, out_shape=(jax.ShapeDtypeStruct((cells, 4, sl...  4.81 us
  transfers between devices with their start and end apart: 16, of which 8 were waited for; matrix products, arithmetic and copies ran while one was open for 0% of the time, Pallas kernels for 4%

commit v1 on v0

--- a/solution.py
+++ b/solution.py
@@ -15,6 +15,7 @@
 
 BLOCK = 128
 TILE = 8
+NEAR = 3
 BF16 = jnp.bfloat16
 F32 = jnp.float32
 
@@ -28,14 +29,20 @@
     return high, (a - high.astype(F32)).astype(BF16)
 
 
-def three_pass(a, b, dims):
+def three_pass(a, b, axis_a):
     a_high, a_low = two_parts(a)
     b_high, b_low = two_parts(b)
-    return matmul(a_high, b_high, dims) + (matmul(a_high, b_low, dims) + matmul(a_low, b_high, dims))
+    left = jnp.concatenate([a_high, a_high, a_low], axis=axis_a)
+    right = jnp.concatenate([b_high, b_low, b_high], axis=0)
+    return matmul(left, right, ((axis_a,), (0,)))
 
 
 def spread(row, sublane):
     return jnp.broadcast_to(row[sublane : sublane + 1, :], row.shape)
+
+
+def columns_of(tile, group):
+    return [jnp.broadcast_to(tile[:, k : k + 1], tile.shape) for k in range(TILE * group, TILE * (group + 1))]
 
 
 def factor_block(tiles):
@@ -43,9 +50,13 @@
     sub = lax.broadcasted_iota(jnp.int32, shape, 0)
     lane = lax.broadcasted_iota(jnp.int32, shape, 1)
     tiles, rows_out, pivots = list(tiles), [], []
+    cols = columns_of(tiles[0], 0)
     for j, tile in enumerate(tiles):
-        first = TILE * j
-        cols = [jnp.broadcast_to(tile[:, first + k : first + k + 1], shape) for k in range(TILE)]
+        first, more = TILE * j, j + 1 < len(tiles)
+        if more:
+            ahead, cols_next, ahead_next = (
+                columns_of(tile, j + 1), columns_of(tiles[j + 1], j), columns_of(tiles[j + 1], j + 1)
+            )
         inverse, ratio, rows = [], {}, []
         pivot = jnp.zeros(shape, F32)
         for k in range(TILE):
@@ -57,17 +68,38 @@
                 cols[m] = cols[m] - cols[k] * ratio[k, m]
             rows.append(spread(tile, k) + jnp.where(lane == first + k, 1.0, 0.0))
             tile = tile - jnp.where(sub > k, cols[k] * inverse[k], 0.0) * rows[k]
-        for i in range(j + 1, len(tiles)):
-            cols = [jnp.broadcast_to(tiles[i][:, first + k : first + k + 1], shape) for k in range(TILE)]
-            below = tiles[i]
+            if more:
+                for m in range(TILE):
+                    part = spread(ahead[m], k) * inverse[k]
+                    ahead[m] = ahead[m] - cols[k] * part
+                    ahead_next[m] = ahead_next[m] - cols_next[k] * part
+                for m in range(k + 1, TILE):
+                    cols_next[m] = cols_next[m] - cols_next[k] * ratio[k, m]
+                tiles[j + 1] = tiles[j + 1] - (cols_next[k] * inverse[k]) * rows[k]
+        root = lax.rsqrt(pivot)
+        unit = jnp.where(lane < sub + first, tile, jnp.where(lane == sub + first, 1.0, 0.0)) * root
+        rows_out.append(unit)
+        near = min(j + 1 + NEAR, len(tiles))
+        if near < len(tiles):
+            scaled = jnp.where(lane < first + TILE, unit, tile * root)
+            high, low = [part.astype(F32) for part in two_parts(scaled)]
+            left = jnp.concatenate([high, high, low], axis=0)[:, TILE * near :]
+            right = jnp.concatenate([high, low, high], axis=0)
+            update = matmul(left.astype(BF16), right.astype(BF16), ((0,), (0,)))
+            group = jnp.logical_and(lane >= first, lane < first + TILE)
+            for i in range(near, len(tiles)):
+                at = TILE * (i - near)
+                tiles[i] = jnp.where(group, 0.0, tiles[i]) - update[at : at + TILE, :]
+        for i in range(j + 2, near):
+            low, below = columns_of(tiles[i], j), tiles[i]
             for k in range(TILE):
                 for m in range(k + 1, TILE):
-                    cols[m] = cols[m] - cols[k] * ratio[k, m]
-                below = below - (cols[k] * inverse[k]) * rows[k]
+                    low[m] = low[m] - low[k] * ratio[k, m]
+                below = below - (low[k] * inverse[k]) * rows[k]
             tiles[i] = below
-        unit = jnp.where(lane < sub + first, tile, jnp.where(lane == sub + first, 1.0, 0.0))
-        rows_out.append(unit * lax.rsqrt(pivot))
         pivots.append(pivot)
+        if more:
+            cols = ahead_next
     return rows_out, pivots
 
 
@@ -81,22 +113,16 @@
             pivots[pl.ds(top + TILE * i, TILE), :] = pivot_tiles[i]
             small[TILE * i : TILE * (i + 1), :] = rows_out[i]
         inverse = small[...]
-
-        def scale(col, carry):
-            cols = pl.ds(pl.multiple_of(col * BLOCK, BLOCK), BLOCK)
-            work[own, cols] = three_pass(inverse, work[own, cols], ((1,), (0,)))
-            return carry
-
-        lax.fori_loop(0, total, scale, 0)
+        work[own, :] = three_pass(inverse, work[own, :], 1)
         work[own, own] = inverse
-
-        def trail(row, carry):
-            rows = pl.ds(pl.multiple_of(row * BLOCK, BLOCK), BLOCK)
-            work[rows, own] = jnp.zeros((BLOCK, BLOCK), F32)
-            work[rows, :] = work[rows, :] - three_pass(work[own, rows].T, work[own, :], ((1,), (0,)))
-            return carry
-
-        lax.fori_loop(step + 1, total, trail, 0)
+        for now in range(total - 1):
+
+            @pl.when(step == now)
+            def _():
+                here, rest = slice(now * BLOCK, (now + 1) * BLOCK), slice((now + 1) * BLOCK, total * BLOCK)
+                work[rest, here] = jnp.zeros(((total - 1 - now) * BLOCK, BLOCK), F32)
+                work[rest, :] = work[rest, :] - three_pass(work[here, rest], work[here, :], 0)
+
         return carry
 
     lax.fori_loop(0, total, one_block, 0)

time: 148 us -> 124 us (0.84)
  Pallas kernels: 67.8 us -> 42.9 us
    pallas_call x3, Pallas kernels: 59.7 us -> 34.9 us  [call(): pl.pallas_call(unpacked, out_shape=out_shapes, scratch_shapes=scratch, co...]
  transfers between devices with their start and end apart: 16 -> 16, of which waited for: 8 -> 8; matrix products, arithmetic and copies ran while one was open for 0% -> 0% of each run, Pallas kernels for 4% -> 5%
where the time goes in v1:
time: 124 us; the launch traced here: 123 us
  waiting for transfers between devices  48.8 us (39%)
  Pallas kernels  42.9 us (35%)
  starting transfers between devices  27.6 us (22%)
  local copies, waits for them, and re-layouts  1.88 us (2%)
  other arithmetic  1.48 us (1%)
    pallas_call x3, Pallas kernels, call(): pl.pallas_call(unpacked, out_shape=out_shapes, scratch_shapes=scratch, co...  34.9 us
    ppermute x6, waiting for transfers between devices, flip(): lax.ppermute(array, axis, [(i, i ^ bit) for i in range(lax.axis_size(axis...  25.7 us
    ppermute x3, waiting for transfers between devices, orthonormalize(): lax.ppermute(total, 'space', [(i, (i + k) % pieces) for i in range(pieces)])  13.8 us
    ppermute x3, waiting for transfers between devices, orthonormalize(): lax.ppermute(parts[k], 'space', [(i, (i + k) % pieces) for i in range(pie...  9.21 us
    ppermute x6, starting transfers between devices, flip(): lax.ppermute(array, axis, [(i, i ^ bit) for i in range(lax.axis_size(axis...  9.13 us
    ppermute x3, starting transfers between devices, orthonormalize(): lax.ppermute(total, 'space', [(i, (i + k) % pieces) for i in range(pieces)])  5.94 us
    ppermute x3, starting transfers between devices, orthonormalize(): lax.ppermute(parts[k], 'space', [(i, (i + k) % pieces) for i in range(pie...  5.78 us
    pallas_call x1, Pallas kernels, dynamics(): pl.pallas_call(path_kernel, out_shape=(jax.ShapeDtypeStruct((cells, 4, sl...  4.81 us
  transfers between devices with their start and end apart: 16, of which 8 were waited for; matrix products, arithmetic and copies ran while one was open for 0% of the time, Pallas kernels for 5%

profile of v1, /device:TPU:7, one launch (start us, length us, event | category | flops | bytes accessed | tf_op | source)
XLA Modules:
  0.0 123.3 jit_solution(6733313179083497954)
XLA Ops:
  0.6 0.7 compare_convert_fusion
  1.4 0.7 pad_maximum_fusion.1.raw_ref
  2.1 3.3 %collective-permute-start.1 = (f32[2,5,128]{2,1,0:T(8,128)S(1)}, f32[2,5,128]{2,1,0:T(8,128)S(1)}, u32[]{:S(2)}, u32[]{:S(2)}) collective-permute-start(f32[2,5,128]{2,1,0:T(8,128)S(1)} %pad_maximum_fusion.1.raw_ref), channel_id=1, source_target_pairs={{4,0},{8,4},{12,8},{0,12},{5,1},{9,5},{13,9},{1,13},{6,2},{10,6},{... | collective-permute-start | bytes 15368 | tf_op jit(solution)/shard_map/ppermute | solution.py:475
  5.4 0.0 collective-permute-start
  5.4 1.2 copy-done
  6.6 0.7 copy-done.1
  7.3 1.1 shard_map.68
  8.4 0.1 collective-permute-start.2
  8.4 3.3 %collective-permute-start.3 = (bf16[10,32,256]{2,1,0:T(8,128)(2,1)S(1)}, bf16[10,32,256]{2,1,0:T(8,128)(2,1)S(1)}, u32[]{:S(2)}, u32[]{:S(2)}) collective-permute-start(bf16[10,32,256]{2,1,0:T(8,128)(2,1)S(1)} %get-tuple-element.18), channel_id=1, source_target_pairs={{4,0},{8,4},{12,8},{0,12},{5,1},{9,5},{13,9},{1,13},{6,2},{10,6},{... | collective-permute-start | bytes 491528 | tf_op jit(solution)/shard_map/ppermute | solution.py:485
  11.7 0.0 collective-permute-done.1.high_ref
  11.7 4.8 %shard_map.67 = (f32[2,4,128]{2,1,0:T(4,128)}, bf16[3,6,14,32,128]{4,3,2,1,0:T(8,128)(2,1)S(1)}) custom-call(f32[2,5,128]{2,1,0:T(8,128)S(1)} %pad_maximum_fusion.1.raw_ref, f32[2,5,128]{2,1,0:T(8,128)S(1)} %collective-permute-done.low_ref, f32[2,5,128]{2,1,0:T(8,128)S(1)} %collective-permute-done.1.high_ref), custom_call_target="tpu_custom_call" | custom-call | flops 4000000000 | bytes 4000000 | tf_op jit(solution)/shard_map/pallas_call | solution.py:486
  16.6 2.2 %shard_map.69 = bf16[2,4,128,256]{3,2,1,0:T(8,128)(2,1)S(1)} custom-call(f32[2,5,128]{2,1,0:T(8,128)S(1)} %pad_maximum_fusion.1.raw_ref, bf16[3,6,14,32,128]{4,3,2,1,0:T(8,128)(2,1)S(1)} %get-tuple-element.15.k_ref, f32[4,8,32,256]{3,2,1,0:T(8,128)S(1)} %get-tuple-element.16.state_ref, bf16[10,32,256]{2,1,0:T(8,128)(2,1)S(1)} %collective-permute-done.2.low_ref, ...), custom_call_target="tpu_custom_call" | custom-call | tf_op jit(solution)/shard_map/pallas_call | solution.py:496
  18.7 0.3 collective-permute-start.5
  19.1 2.4 %collective-permute-start.4 = (bf16[1024,256]{1,0:T(8,128)(2,1)S(1)}, bf16[1024,256]{1,0:T(8,128)(2,1)S(1)}, u32[]{:S(2)}, u32[]{:S(2)}) collective-permute-start(bf16[1024,256]{1,0:T(8,128)(2,1)S(1)} %bitcast.8), channel_id=1, source_target_pairs={{0,1},{1,0},{2,3},{3,2},{4,5},{5,4},{6,7},{7,6},{8,9},{9,8},{10,11... | collective-permute-start | bytes 1572872 | tf_op jit(solution)/shard_map/ppermute | solution.py:224
  21.5 8.6 %collective-permute-done.5.refs_2_.refs_6_ = bf16[1024,256]{1,0:T(8,128)(2,1)S(1)} collective-permute-done((bf16[1024,256]{1,0:T(8,128)(2,1)S(1)}, bf16[1024,256]{1,0:T(8,128)(2,1)S(1)}, u32[]{:S(2)}, u32[]{:S(2)}) %collective-permute-start.5) | collective-permute-done | bytes 524320 | tf_op jit(solution)/shard_map/ppermute | solution.py:224
  30.1 3.1 %collective-permute-start.6 = (bf16[1024,256]{1,0:T(8,128)(2,1)S(1)}, bf16[1024,256]{1,0:T(8,128)(2,1)S(1)}, u32[]{:S(2)}, u32[]{:S(2)}) collective-permute-start(bf16[1024,256]{1,0:T(8,128)(2,1)S(1)} %collective-permute-done.5.refs_2_.refs_6_), channel_id=1, source_target_pairs={{0,1},{1,0},{2,3},{3,2},{4,5},{5,4},{6,7},{7,6},{8,9},{9,8},{10,11... | collective-permute-start | bytes 1572872 | tf_op jit(solution)/shard_map/ppermute | solution.py:224
  33.1 1.5 %collective-permute-done.6.refs_3_.refs_7_ = bf16[1024,256]{1,0:T(8,128)(2,1)S(1)} collective-permute-done((bf16[1024,256]{1,0:T(8,128)(2,1)S(1)}, bf16[1024,256]{1,0:T(8,128)(2,1)S(1)}, u32[]{:S(2)}, u32[]{:S(2)}) %collective-permute-start.6) | collective-permute-done | bytes 524320 | tf_op jit(solution)/shard_map/ppermute | solution.py:224
  34.7 1.2 shard_map.70
  35.9 3.6 %collective-permute-start.7 = (f32[160,256]{1,0:T(8,128)S(1)}, f32[160,256]{1,0:T(8,128)S(1)}, u32[]{:S(2)}, u32[]{:S(2)}) collective-permute-start(f32[160,256]{1,0:T(8,128)S(1)} %get-tuple-element.20), channel_id=1, source_target_pairs={{0,4},{4,8},{8,12},{12,0},{1,5},{5,9},{9,13},{13,1},{2,6},{6,10},{... | collective-permute-start | bytes 491528 | tf_op jit(solution)/shard_map/ppermute | solution.py:251
  39.5 2.2 %collective-permute-start.9 = (f32[160,256]{1,0:T(8,128)S(1)}, f32[160,256]{1,0:T(8,128)S(1)}, u32[]{:S(2)}, u32[]{:S(2)}) collective-permute-start(f32[160,256]{1,0:T(8,128)S(1)} %get-tuple-element.22), channel_id=1, source_target_pairs={{0,12},{4,0},{8,4},{12,8},{1,13},{5,1},{9,5},{13,9},{2,14},{6,2},{... | collective-permute-start | bytes 491528 | tf_op jit(solution)/shard_map/ppermute | solution.py:251
  41.7 1.5 %collective-permute-done.7.refs_1_ = f32[160,256]{1,0:T(8,128)S(1)} collective-permute-done((f32[160,256]{1,0:T(8,128)S(1)}, f32[160,256]{1,0:T(8,128)S(1)}, u32[]{:S(2)}, u32[]{:S(2)}) %collective-permute-start.7) | collective-permute-done | bytes 163872 | tf_op jit(solution)/shard_map/ppermute | solution.py:251
  43.2 7.7 %collective-permute-done.8.refs_2_ = f32[160,256]{1,0:T(8,128)S(1)} collective-permute-done((f32[160,256]{1,0:T(8,128)S(1)}, f32[160,256]{1,0:T(8,128)S(1)}, u32[]{:S(2)}, u32[]{:S(2)}) %collective-permute-start.8) | collective-permute-done | bytes 163872 | tf_op jit(solution)/shard_map/ppermute | solution.py:251
  50.9 5.6 %collective-permute-start.12 = (f32[160,256]{1,0:T(8,128)S(1)}, f32[160,256]{1,0:T(8,128)S(1)}, u32[]{:S(2)}, u32[]{:S(2)}) collective-permute-start(f32[160,256]{1,0:T(8,128)S(1)} %shard_map.71), channel_id=1, source_target_pairs={{0,12},{4,0},{8,4},{12,8},{1,13},{5,1},{9,5},{13,9},{2,14},{6,2},{... | collective-permute-start | bytes 491528 | tf_op jit(solution)/shard_map/ppermute | solution.py:255
  56.5 0.4 collective-permute-start.10
  56.9 2.4 %collective-permute-done.12 = f32[160,256]{1,0:T(8,128)S(1)} collective-permute-done((f32[160,256]{1,0:T(8,128)S(1)}, f32[160,256]{1,0:T(8,128)S(1)}, u32[]{:S(2)}, u32[]{:S(2)}) %collective-permute-start.12) | collective-permute-done | bytes 163872 | tf_op jit(solution)/shard_map/ppermute | solution.py:255
  59.3 11.5 %collective-permute-done.11 = f32[160,256]{1,0:T(8,128)S(1)} collective-permute-done((f32[160,256]{1,0:T(8,128)S(1)}, f32[160,256]{1,0:T(8,128)S(1)}, u32[]{:S(2)}, u32[]{:S(2)}) %collective-permute-start.11) | collective-permute-done | bytes 163872 | tf_op jit(solution)/shard_map/ppermute | solution.py:255
  70.8 0.3 collective-permute-start.14
  71.1 1.2 collective-permute-start.13
  72.3 13.9 %collective-permute-done.14.refs_2_ = f32[4,160,256]{2,1,0:T(8,128)S(1)} collective-permute-done((f32[4,160,256]{2,1,0:T(8,128)S(1)}, f32[4,160,256]{2,1,0:T(8,128)S(1)}, u32[]{:S(2)}, u32[]{:S(2)}) %collective-permute-start.14) | collective-permute-done | bytes 655392 | tf_op jit(solution)/shard_map/ppermute | solution.py:224
  86.2 1.8 %collective-permute-start.15 = (f32[4,160,256]{2,1,0:T(8,128)S(1)}, f32[4,160,256]{2,1,0:T(8,128)S(1)}, u32[]{:S(2)}, u32[]{:S(2)}) collective-permute-start(f32[4,160,256]{2,1,0:T(8,128)S(1)} %collective-permute-done.14.refs_2_), channel_id=1, source_target_pairs={{0,1},{1,0},{2,3},{3,2},{4,5},{5,4},{6,7},{7,6},{8,9},{9,8},{10,11... | collective-permute-start | bytes 1966088 | tf_op jit(solution)/shard_map/ppermute | solution.py:224
  88.0 1.7 %collective-permute-done.15.refs_3_ = f32[4,160,256]{2,1,0:T(8,128)S(1)} collective-permute-done((f32[4,160,256]{2,1,0:T(8,128)S(1)}, f32[4,160,256]{2,1,0:T(8,128)S(1)}, u32[]{:S(2)}, u32[]{:S(2)}) %collective-permute-start.15) | collective-permute-done | bytes 655392 | tf_op jit(solution)/shard_map/ppermute | solution.py:224
  89.7 33.6 %shard_map.72 = (f32[1024,256]{1,0:T(8,128)}, f32[1,256]{1,0:T(1,128)}) custom-call(f32[4,160,256]{2,1,0:T(8,128)S(1)} %pad_maximum_fusion.refs_0_, f32[4,160,256]{2,1,0:T(8,128)S(1)} %collective-permute-done.13.refs_1_, f32[4,160,256]{2,1,0:T(8,128)S(1)} %collective-permute-done.14.refs_2_, f32[4,160,256]{2,1,0:T(8,128)S(1)} %collective-permute-done.15.refs_3_, ...), custom_call_target="tpu_custom_call" | custom-call | tf_op jit(solution)/shard_map/pallas_call | solution.py:215
  (13 shorter events, 0.1 us)
Async XLA Ops:
  2.1 9.7 %collective-permute-start.1 = (f32[2,5,128]{2,1,0:T(8,128)S(1)}, f32[2,5,128]{2,1,0:T(8,128)S(1)}, u32[]{:S(2)}, u32[]{:S(2)}) collective-permute-start(f32[2,5,128]{2,1,0:T(8,128)S(1)} %pad_maximum_fusion.1.raw_ref), channel_id=1, source_target_pairs={{4,0},{8,4},{12,8},{0,12},{5,1},{9,5},{13,9},{1,13},{6,2},{10,6},{... | collective-permute-start | bytes 15368 | tf_op jit(solution)/shard_map/ppermute | solution.py:475
  5.4 6.4 %collective-permute-start = (f32[2,5,128]{2,1,0:T(8,128)S(1)}, f32[2,5,128]{2,1,0:T(8,128)S(1)}, u32[]{:S(2)}, u32[]{:S(2)}) collective-permute-start(f32[2,5,128]{2,1,0:T(8,128)S(1)} %pad_maximum_fusion.1.raw_ref), channel_id=1, source_target_pairs={{0,4},{4,8},{8,12},{12,0},{1,5},{5,9},{9,13},{13,1},{2,6},{6,10},{... | collective-permute-start | bytes 15368 | tf_op jit(solution)/shard_map/ppermute | solution.py:475
  5.4 1.2 copy-start
  6.6 0.7 copy-start.1
  8.4 8.2 %collective-permute-start.2 = (bf16[10,32,256]{2,1,0:T(8,128)(2,1)S(1)}, bf16[10,32,256]{2,1,0:T(8,128)(2,1)S(1)}, u32[]{:S(2)}, u32[]{:S(2)}) collective-permute-start(bf16[10,32,256]{2,1,0:T(8,128)(2,1)S(1)} %get-tuple-element.17), channel_id=1, source_target_pairs={{0,4},{4,8},{8,12},{12,0},{1,5},{5,9},{9,13},{13,1},{2,6},{6,10},{... | collective-permute-start | bytes 491528 | tf_op jit(solution)/shard_map/ppermute | solution.py:485
  8.4 8.1 %collective-permute-start.3 = (bf16[10,32,256]{2,1,0:T(8,128)(2,1)S(1)}, bf16[10,32,256]{2,1,0:T(8,128)(2,1)S(1)}, u32[]{:S(2)}, u32[]{:S(2)}) collective-permute-start(bf16[10,32,256]{2,1,0:T(8,128)(2,1)S(1)} %get-tuple-element.18), channel_id=1, source_target_pairs={{4,0},{8,4},{12,8},{0,12},{5,1},{9,5},{13,9},{1,13},{6,2},{10,6},{... | collective-permute-start | bytes 491528 | tf_op jit(solution)/shard_map/ppermute | solution.py:485
  18.7 11.3 %collective-permute-start.5 = (bf16[1024,256]{1,0:T(8,128)(2,1)S(1)}, bf16[1024,256]{1,0:T(8,128)(2,1)S(1)}, u32[]{:S(2)}, u32[]{:S(2)}) collective-permute-start(bf16[1024,256]{1,0:T(8,128)(2,1)S(1)} %bitcast.7), channel_id=1, source_target_pairs={{0,2},{1,3},{2,0},{3,1},{4,6},{5,7},{6,4},{7,5},{8,10},{9,11},{10,... | collective-permute-start | bytes 1572872 | tf_op jit(solution)/shard_map/ppermute | solution.py:224
  19.1 14.1 %collective-permute-start.4 = (bf16[1024,256]{1,0:T(8,128)(2,1)S(1)}, bf16[1024,256]{1,0:T(8,128)(2,1)S(1)}, u32[]{:S(2)}, u32[]{:S(2)}) collective-permute-start(bf16[1024,256]{1,0:T(8,128)(2,1)S(1)} %bitcast.8), channel_id=1, source_target_pairs={{0,1},{1,0},{2,3},{3,2},{4,5},{5,4},{6,7},{7,6},{8,9},{9,8},{10,11... | collective-permute-start | bytes 1572872 | tf_op jit(solution)/shard_map/ppermute | solution.py:224
  30.1 4.6 %collective-permute-start.6 = (bf16[1024,256]{1,0:T(8,128)(2,1)S(1)}, bf16[1024,256]{1,0:T(8,128)(2,1)S(1)}, u32[]{:S(2)}, u32[]{:S(2)}) collective-permute-start(bf16[1024,256]{1,0:T(8,128)(2,1)S(1)} %collective-permute-done.5.refs_2_.refs_6_), channel_id=1, source_target_pairs={{0,1},{1,0},{2,3},{3,2},{4,5},{5,4},{6,7},{7,6},{8,9},{9,8},{10,11... | collective-permute-start | bytes 1572872 | tf_op jit(solution)/shard_map/ppermute | solution.py:224
  35.9 7.3 %collective-permute-start.7 = (f32[160,256]{1,0:T(8,128)S(1)}, f32[160,256]{1,0:T(8,128)S(1)}, u32[]{:S(2)}, u32[]{:S(2)}) collective-permute-start(f32[160,256]{1,0:T(8,128)S(1)} %get-tuple-element.20), channel_id=1, source_target_pairs={{0,4},{4,8},{8,12},{12,0},{1,5},{5,9},{9,13},{13,1},{2,6},{6,10},{... | collective-permute-start | bytes 491528 | tf_op jit(solution)/shard_map/ppermute | solution.py:251
  39.5 11.4 %collective-permute-start.8 = (f32[160,256]{1,0:T(8,128)S(1)}, f32[160,256]{1,0:T(8,128)S(1)}, u32[]{:S(2)}, u32[]{:S(2)}) collective-permute-start(f32[160,256]{1,0:T(8,128)S(1)} %get-tuple-element.21), channel_id=1, source_target_pairs={{0,8},{4,12},{8,0},{12,4},{1,9},{5,13},{9,1},{13,5},{2,10},{6,14},... | collective-permute-start | bytes 491528 | tf_op jit(solution)/shard_map/ppermute | solution.py:251
  39.5 11.4 %collective-permute-start.9 = (f32[160,256]{1,0:T(8,128)S(1)}, f32[160,256]{1,0:T(8,128)S(1)}, u32[]{:S(2)}, u32[]{:S(2)}) collective-permute-start(f32[160,256]{1,0:T(8,128)S(1)} %get-tuple-element.22), channel_id=1, source_target_pairs={{0,12},{4,0},{8,4},{12,8},{1,13},{5,1},{9,5},{13,9},{2,14},{6,2},{... | collective-permute-start | bytes 491528 | tf_op jit(solution)/shard_map/ppermute | solution.py:251
  50.9 8.3 %collective-permute-start.12 = (f32[160,256]{1,0:T(8,128)S(1)}, f32[160,256]{1,0:T(8,128)S(1)}, u32[]{:S(2)}, u32[]{:S(2)}) collective-permute-start(f32[160,256]{1,0:T(8,128)S(1)} %shard_map.71), channel_id=1, source_target_pairs={{0,12},{4,0},{8,4},{12,8},{1,13},{5,1},{9,5},{13,9},{2,14},{6,2},{... | collective-permute-start | bytes 491528 | tf_op jit(solution)/shard_map/ppermute | solution.py:255
  56.5 14.2 %collective-permute-start.11 = (f32[160,256]{1,0:T(8,128)S(1)}, f32[160,256]{1,0:T(8,128)S(1)}, u32[]{:S(2)}, u32[]{:S(2)}) collective-permute-start(f32[160,256]{1,0:T(8,128)S(1)} %shard_map.71), channel_id=1, source_target_pairs={{0,8},{4,12},{8,0},{12,4},{1,9},{5,13},{9,1},{13,5},{2,10},{6,14},... | collective-permute-start | bytes 491528 | tf_op jit(solution)/shard_map/ppermute | solution.py:255
  56.5 14.2 %collective-permute-start.10 = (f32[160,256]{1,0:T(8,128)S(1)}, f32[160,256]{1,0:T(8,128)S(1)}, u32[]{:S(2)}, u32[]{:S(2)}) collective-permute-start(f32[160,256]{1,0:T(8,128)S(1)} %shard_map.71), channel_id=1, source_target_pairs={{0,4},{4,8},{8,12},{12,0},{1,5},{5,9},{9,13},{13,1},{2,6},{6,10},{... | collective-permute-start | bytes 491528 | tf_op jit(solution)/shard_map/ppermute | solution.py:255
  70.8 15.4 %collective-permute-start.14 = (f32[4,160,256]{2,1,0:T(8,128)S(1)}, f32[4,160,256]{2,1,0:T(8,128)S(1)}, u32[]{:S(2)}, u32[]{:S(2)}) collective-permute-start(f32[4,160,256]{2,1,0:T(8,128)S(1)} %pad_maximum_fusion.refs_0_), channel_id=1, source_target_pairs={{0,2},{1,3},{2,0},{3,1},{4,6},{5,7},{6,4},{7,5},{8,10},{9,11},{10,... | collective-permute-start | bytes 1966088 | tf_op jit(solution)/shard_map/ppermute | solution.py:224
  71.1 16.9 %collective-permute-start.13 = (f32[4,160,256]{2,1,0:T(8,128)S(1)}, f32[4,160,256]{2,1,0:T(8,128)S(1)}, u32[]{:S(2)}, u32[]{:S(2)}) collective-permute-start(f32[4,160,256]{2,1,0:T(8,128)S(1)} %pad_maximum_fusion.refs_0_), channel_id=1, source_target_pairs={{0,1},{1,0},{2,3},{3,2},{4,5},{5,4},{6,7},{7,6},{8,9},{9,8},{10,11... | collective-permute-start | bytes 1966088 | tf_op jit(solution)/shard_map/ppermute | solution.py:224
  86.2 3.6 %collective-permute-start.15 = (f32[4,160,256]{2,1,0:T(8,128)S(1)}, f32[4,160,256]{2,1,0:T(8,128)S(1)}, u32[]{:S(2)}, u32[]{:S(2)}) collective-permute-start(f32[4,160,256]{2,1,0:T(8,128)S(1)} %collective-permute-done.14.refs_2_), channel_id=1, source_target_pairs={{0,1},{1,0},{2,3},{3,2},{4,5},{5,4},{6,7},{7,6},{8,9},{9,8},{10,11... | collective-permute-start | bytes 1966088 | tf_op jit(solution)/shard_map/ppermute | solution.py:224

commit v2 on v1

--- a/solution.py
+++ b/solution.py
@@ -128,28 +128,45 @@
     lax.fori_loop(0, total, one_block, 0)
 
 
-def gram_kernel(shards, pieces, bc, x_refs, out_refs, part):
+def share_pair(k, me, half, x_own, x_far, out_ref, rows):
+    lower = me < (me ^ k)
+
+    @pl.when(lower)
+    def _():
+        out_ref[rows, :] = matmul(x_own[:, 0:half], x_far[...], ((0,), (0,)))
+
+    @pl.when(jnp.logical_not(lower))
+    def _():
+        out_ref[rows, :] = matmul(x_far[:, half:], x_own[...], ((0,), (0,)))
+
+
+def deal(part, out_refs):
+    size, pieces = out_refs[0].shape[0], len(out_refs)
+    for k in range(pieces):
+        start = pl.multiple_of(lax.rem(lax.axis_index("space") + k, pieces) * size, 8)
+        out_refs[k][...] = part[pl.ds(start, size), :]
+
+
+def near_gram_kernel(x_refs, out_refs, part):
     me = lax.axis_index("tangent")
-    here = lax.axis_index("space")
-    half = bc // 2
+    half = x_refs[0].shape[1] // 2
+    quarter = half // 2
     own = x_refs[0][...]
-    part[0:bc, :] = matmul(own, own, ((0,), (0,)))
-    for k in range(1, shards):
-        rows = slice(bc + (k - 1) * half, bc + k * half)
-        lower = me < (me ^ k)
-
-        @pl.when(lower)
-        def _():
-            part[rows, :] = matmul(x_refs[0][:, 0:half], x_refs[k][...], ((0,), (0,)))
-
-        @pl.when(jnp.logical_not(lower))
-        def _():
-            part[rows, :] = matmul(x_refs[k][:, half:bc], x_refs[0][...], ((0,), (0,)))
-
-    size = part.shape[0] // pieces
-    for k in range(pieces):
-        start = pl.multiple_of(lax.rem(here + k, pieces) * size, 16)
-        out_refs[k][...] = part[pl.ds(start, size), :]
+    part[0:half, :] = matmul(own[:, 0:half], own, ((0,), (0,)))
+    last = matmul(own[:, half:], own[:, half:], ((0,), (0,)))
+    part[half : half + quarter, 0:half] = last[0:quarter]
+    part[half : half + quarter, half:] = last[quarter:]
+    for k in range(1, len(x_refs)):
+        at = half + quarter + (k - 1) * half
+        share_pair(k, me, half, x_refs[0], x_refs[k], part, slice(at, at + half))
+    deal(part, out_refs)
+
+
+def far_gram_kernel(x_own, x_refs, out_refs, part):
+    bc = x_own[0].shape[1]
+    for k in range(len(x_refs)):
+        part[k * bc : (k + 1) * bc, :] = matmul(x_refs[k][...], x_own[0][...], ((0,), (0,)))
+    deal(part, out_refs)
 
 
 def sum_kernel(in_refs, out_ref):
@@ -159,53 +176,138 @@
     out_ref[...] = total
 
 
-def solve_kernel(shards, pieces, bc, scale, g_refs, x_refs, out_ref, log_ref, work, pivots, small, part):
+def collect(g_ref, scale, part):
+    pieces, size = g_ref.shape[0], g_ref.shape[1]
+    for j in range(pieces):
+        start = pl.multiple_of(lax.rem(lax.axis_index("space") + pieces - j, pieces) * size, 8)
+        part[pl.ds(start, size), :] = g_ref[j] * scale
+
+
+def place_pairs(peer, count, offset, part, work):
+    bc = part.shape[1]
+    half = bc // 2
+    for j in range(1, count):
+        other = peer ^ j
+        low, high = jnp.minimum(peer, other), jnp.maximum(peer, other)
+        top = pl.multiple_of(low * bc + jnp.where(peer == high, half, 0), half)
+        at = offset + (j - 1) * half
+        work[pl.ds(top, half), pl.ds(pl.multiple_of(high * bc, BLOCK), bc)] = part[at : at + half, :]
+
+
+def near_blocks(g_refs, upper, scale, part, work):
     me = lax.axis_index("tangent")
-    here = lax.axis_index("space")
+    shards = len(g_refs)
+    inner = shards // 2
+    bc = part.shape[1]
     half = bc // 2
-    size = part.shape[0] // pieces
+    quarter = half // 2
     for k in range(shards):
-        peer = me ^ k
-        for j in range(pieces):
-            start = pl.multiple_of(lax.rem(here + pieces - j, pieces) * size, 16)
-            part[pl.ds(start, size), :] = g_refs[k][j] * scale
-        cols = pl.ds(pl.multiple_of(peer * bc, BLOCK), bc)
-        work[cols, cols] = part[0:bc, :]
-        for j in range(1, shards):
-            other = peer ^ j
-            low, high = jnp.minimum(peer, other), jnp.maximum(peer, other)
-            top = pl.multiple_of(low * bc + jnp.where(peer == high, half, 0), half)
-            work[pl.ds(top, half), pl.ds(pl.multiple_of(high * bc, BLOCK), bc)] = part[
-                bc + (j - 1) * half : bc + j * half, :
-            ]
-    eliminate(shards * bc // BLOCK, work, pivots, small)
-    mine = pl.ds(pl.multiple_of(me * bc, BLOCK), bc)
-    row_block = lax.broadcasted_iota(jnp.int32, (bc, bc), 0) // BLOCK
-    col_block = lax.broadcasted_iota(jnp.int32, (bc, bc), 1) // BLOCK
-
-    def times(x_ref, factor):
-        high, low = two_parts(factor)
-        return matmul(x_ref[...], high, ((1,), (1,))) + matmul(x_ref[...], low, ((1,), (1,)))
-
-    out_ref[...] = times(x_refs[0], jnp.where(row_block >= col_block, work[mine, mine], 0.0))
-    for k in range(1, shards):
-        peer = me ^ k
-
-        @pl.when(peer < me)
+        same_half = (me < inner) if (k < inner) != upper else (me >= inner)
+
+        @pl.when(same_half)
         def _():
-            cols = pl.ds(pl.multiple_of(peer * bc, BLOCK), bc)
-            out_ref[...] += times(x_refs[k], work[mine, cols])
-
+            peer = (me ^ k) & (inner - 1)
+            collect(g_refs[k], scale, part)
+            top = pl.multiple_of(peer * bc, BLOCK)
+            work[pl.ds(top, half), pl.ds(top, bc)] = part[0:half, :]
+            if half % BLOCK:
+                full = part[0:half, half:]
+                block = jnp.concatenate([part[half : half + quarter, 0:half], part[half : half + quarter, half:]], axis=0)
+                work[pl.ds(top + half, half), pl.ds(top, bc)] = jnp.concatenate([full.T, block], axis=1)
+            else:
+                right = pl.ds(pl.multiple_of(top + half, BLOCK), half)
+                work[pl.ds(top + half, quarter), right] = part[half : half + quarter, 0:half]
+                work[pl.ds(top + half + quarter, quarter), right] = part[half : half + quarter, half:]
+            place_pairs(peer, inner, half + quarter, part, work)
+
+
+def log_rows(pivots, log_ref):
     eye = lax.broadcasted_iota(jnp.int32, (BLOCK, BLOCK), 0) == lax.broadcasted_iota(jnp.int32, (BLOCK, BLOCK), 1)
-    for a in range(bc // BLOCK):
-        block = pivots[pl.ds(pl.multiple_of(me * bc + a * BLOCK, BLOCK), BLOCK), :]
+    for a in range(pivots.shape[0] // BLOCK):
+        block = pivots[a * BLOCK : (a + 1) * BLOCK, :]
         log_ref[:, a * BLOCK : (a + 1) * BLOCK] = 0.5 * jnp.log(
             jnp.sum(jnp.where(eye, block, 0.0), axis=0, keepdims=True)
         )
 
 
-def call(kernel, counts, out_shapes, scratch, operands):
+def lower_blocks(matrix):
+    row_block = lax.broadcasted_iota(jnp.int32, matrix.shape, 0) // BLOCK
+    col_block = lax.broadcasted_iota(jnp.int32, matrix.shape, 1) // BLOCK
+    return jnp.where(row_block >= col_block, matrix, 0.0)
+
+
+def first_kernel(scale, g_refs, inverse_ref, log_ref, pivots, small, part):
+    near_blocks(g_refs, False, scale, part, inverse_ref)
+    eliminate(inverse_ref.shape[0] // BLOCK, inverse_ref, pivots, small)
+    inverse_ref[...] = lower_blocks(inverse_ref[...])
+    log_rows(pivots, log_ref)
+
+
+def second_kernel(
+    scale, near_refs, far_refs, x_refs, first_ref, first_log, out_ref, log_ref,
+    work, cross, product, mine, logs, pivots, small, near_part, far_part,
+):
+    me = lax.axis_index("tangent")
+    shards = len(x_refs)
+    inner = shards // 2
+    bc = out_ref.shape[1]
+    full = work.shape[0]
+    near_blocks(near_refs, True, scale, near_part, work)
+
+    @pl.when(me < inner)
+    def _():
+        cross[...] = jnp.zeros(cross.shape, F32)
+
+    @pl.when(me >= inner)
+    def _():
+        for k in range(inner):
+            collect(far_refs[k], scale, far_part)
+            cols = pl.ds(pl.multiple_of((me ^ k) * bc - full, BLOCK), bc)
+            for j in range(inner):
+                rows = pl.ds(pl.multiple_of((me ^ k ^ (j + inner)) * bc, BLOCK), bc)
+                cross[rows, cols] = far_part[j * bc : (j + 1) * bc, :]
+
+    cross[...] = three_pass(first_ref[...], cross[...], 1)
+    work[...] = work[...] - three_pass(cross[...], cross[...], 0)
+    product[...] = three_pass(cross[...], first_ref[...], 0)
+    eliminate(full // BLOCK, work, pivots, small)
+    log_rows(pivots, logs)
+    top = pl.multiple_of((me & (inner - 1)) * bc, BLOCK)
+    rows = pl.ds(top, bc)
+
+    @pl.when(me < inner)
+    def _():
+        mine[:, 0:full] = first_ref[rows, :]
+        mine[:, full:] = jnp.zeros((bc, full), F32)
+        log_ref[...] = first_log[:, rows]
+
+    @pl.when(me >= inner)
+    def _():
+        row_block = (lax.broadcasted_iota(jnp.int32, (bc, full), 0) + top) // BLOCK
+        col_block = lax.broadcasted_iota(jnp.int32, (bc, full), 1) // BLOCK
+        own = jnp.where(row_block >= col_block, work[rows, :], 0.0)
+        mine[:, full:] = own
+        mine[:, 0:full] = -three_pass(own, product[...], 1)
+        log_ref[...] = logs[:, rows]
+
+    def times(x_ref, peer):
+        high, low = two_parts(mine[:, pl.ds(pl.multiple_of(peer * bc, BLOCK), bc)])
+        return matmul(x_ref[...], high, ((1,), (1,))) + matmul(x_ref[...], low, ((1,), (1,)))
+
+    out_ref[...] = times(x_refs[0], me)
+    for k in range(1, shards):
+        peer = me ^ k
+
+        @pl.when(peer < me)
+        def _():
+            out_ref[...] += times(x_refs[k], peer)
+
+
+def call(kernel, counts, out_shapes, scratch, operands, cost=None, after=()):
+    inputs, waits = len(operands), len(after)
+
     def unpacked(*refs):
+        refs = refs[:inputs] + refs[inputs + waits :]
         groups, at = [], 0
         for count in counts:
             groups.append(refs[at : at + count])
@@ -215,70 +317,102 @@
     return pl.pallas_call(
         unpacked,
         out_shape=out_shapes,
+        in_specs=[pl.BlockSpec(memory_space=pltpu.VMEM)] * inputs + [pl.BlockSpec(memory_space=pl.ANY)] * waits,
         scratch_shapes=scratch,
+        cost_estimate=cost,
         compiler_params=pltpu.CompilerParams(vmem_limit_bytes=48 * 1024 * 1024),
-    )(*operands)
+    )(*operands, *after)
 
 
 def flip(array, axis, bit):
     return lax.ppermute(array, axis, [(i, i ^ bit) for i in range(lax.axis_size(axis))])
 
 
+def flips(blocks, bits):
+    for bit in bits:
+        blocks = {**blocks, **{k ^ bit: flip(v, "tangent", bit) for k, v in blocks.items()}}
+    return blocks
+
+
+def scatter(parts, count):
+    if len(parts) == 1:
+        return [lax.psum(parts[0], "space")]
+    arrived = [parts[0]]
+    for k in range(1, count):
+        arrived.append(lax.ppermute(parts[k], "space", [(i, (i + k) % count) for i in range(count)]))
+    return arrived
+
+
+def added(arrived, after=()):
+    shape = jax.ShapeDtypeStruct(arrived[0].shape, F32)
+    return call(sum_kernel, (len(arrived),), shape, [], arrived, after=after)
+
+
+def gather(total, count, cuts):
+    around = [total]
+    for k in range(1, cuts):
+        around.append(lax.ppermute(total, "space", [(i, (i + k) % count) for i in range(count)]))
+    return around
+
+
 def orthonormalize(x):
-    shards, pieces = lax.axis_size("tangent"), lax.axis_size("space")
+    shards, count = lax.axis_size("tangent"), lax.axis_size("space")
     rows, bc = x.shape
-    blocks = {0: x}
-    bit = shards // 2
-    while bit:
-        blocks.update({k ^ bit: flip(v, "tangent", bit) for k, v in list(blocks.items())})
-        bit //= 2
-    blocks = [blocks[k] for k in range(shards)]
-    held = bc + (shards - 1) * (bc // 2)
-    direct = pieces <= 8
-    cuts = pieces if direct else 1
-    size = held // cuts
-    piece = jax.ShapeDtypeStruct((size, bc), F32)
-
-    def gram(*refs):
-        gram_kernel(shards, cuts, bc, *refs)
-
-    parts = call(
-        gram, (shards, cuts), (piece,) * cuts, [pltpu.VMEM((held, bc), F32)], blocks
+    half, inner = bc // 2, shards // 2
+    cuts = count if count <= 8 else 1
+    bits = [1 << b for b in reversed(range(inner.bit_length() - 1))]
+    scale = 1.0 / (float(rows) * count)
+    near_rows, far_rows = half + half // 2 + (inner - 1) * half, inner * bc
+
+    def dealt(held):
+        return (jax.ShapeDtypeStruct((held // cuts, bc), F32),) * cuts
+
+    far_own = flip(x, "tangent", inner)
+    near_x = flips({0: x}, bits)
+    near_x = [near_x[k] for k in range(inner)]
+    near = call(near_gram_kernel, (inner, cuts), dealt(near_rows), [pltpu.VMEM((near_rows, bc), F32)], near_x)
+    near = added(scatter(near, count))
+    around = gather(near, count, cuts)
+    far_x = flips({0: lax.optimization_barrier((far_own, near))[0]}, bits)
+    far_x = [far_x[k] for k in range(inner)]
+    far = call(
+        far_gram_kernel,
+        (1, inner, cuts),
+        dealt(far_rows),
+        [pltpu.VMEM((far_rows, bc), F32)],
+        [x] + far_x,
+        after=[near],
     )
-    if direct:
-        arrived = [parts[0]]
-        for k in range(1, pieces):
-            arrived.append(lax.ppermute(parts[k], "space", [(i, (i + k) % pieces) for i in range(pieces)]))
-        total = call(lambda a, out: sum_kernel(a, out), (pieces,), piece, [], arrived)
-        around = [total]
-        for k in range(1, pieces):
-            around.append(lax.ppermute(total, "space", [(i, (i + k) % pieces) for i in range(pieces)]))
-        total = jnp.stack(around)
-    else:
-        total = lax.psum(parts[0], "space")[None]
-    totals = {0: total}
-    bit = shards // 2
-    while bit:
-        totals.update({k ^ bit: flip(v, "tangent", bit) for k, v in list(totals.items())})
-        bit //= 2
-    totals = [totals[k] for k in range(shards)]
-    scale = 1.0 / (float(rows) * pieces)
-
-    def solve(g_refs, x_refs, *refs):
-        solve_kernel(shards, cuts, bc, scale, g_refs, x_refs, *refs)
-
-    full = shards * bc
+    near = jnp.stack(lax.optimization_barrier((around, far[0]))[0])
+    far = added(scatter(far, count), after=[near])
+    far_around = gather(far, count, cuts)
+    near = flips({0: near}, [inner])
+    near[inner] = lax.optimization_barrier((near[inner], far))[0]
+    near = flips(near, bits)
+    near = [near[k] for k in range(shards)]
+    full = inner * bc
+    square, column = pltpu.VMEM((full, full), F32), pltpu.VMEM((full, BLOCK), F32)
+    block, near_part = pltpu.VMEM((BLOCK, BLOCK), F32), pltpu.VMEM((near_rows, bc), F32)
+    first, first_log = call(
+        lambda *refs: first_kernel(scale, *refs),
+        (shards,),
+        (jax.ShapeDtypeStruct((full, full), F32), jax.ShapeDtypeStruct((1, full), F32)),
+        [column, block, near_part],
+        near,
+        cost=pl.CostEstimate(flops=16 * 10**9, bytes_accessed=4 * 10**6, transcendentals=0),
+    )
+    far_around = lax.optimization_barrier((far_around, first_log))[0]
+    far = flips({0: jnp.stack(far_around)}, bits)
+    far = [far[k] for k in range(inner)]
     out, logs = call(
-        solve,
-        (shards, shards),
+        lambda *refs: second_kernel(scale, *refs),
+        (shards, inner, shards),
         (jax.ShapeDtypeStruct((rows, bc), F32), jax.ShapeDtypeStruct((1, bc), F32)),
         [
-            pltpu.VMEM((full, full), F32),
-            pltpu.VMEM((full, BLOCK), F32),
-            pltpu.VMEM((BLOCK, BLOCK), F32),
-            pltpu.VMEM((held, bc), F32),
+            square, square, square, pltpu.VMEM((bc, 2 * full), F32), pltpu.VMEM((1, full), F32),
+            column, block, near_part, pltpu.VMEM((far_rows, bc), F32),
         ],
-        totals + blocks,
+        near + far + near_x + far_x + [first, first_log],
     )
     return out, logs[0]
 

time: 124 us -> 101 us (0.81)
  waiting for transfers between devices: 48.8 us -> 22.7 us
  starting transfers between devices: 27.6 us -> 30.2 us
    ppermute x6 -> x7, waiting for transfers between devices: 25.7 us -> 4.38 us  [flip(): lax.ppermute(array, axis, [(i, i ^ bit) for i in range(lax.axis_size(axis...]
    ppermute x6 -> x12, waiting for transfers between devices: 23.1 us -> 18.3 us  [the longest x6 10.9 us: scatter(): lax.ppermute(parts[k], 'space', [(i, (i + k) % count) for i in range(coun...]
    ppermute x6 -> x12, starting transfers between devices: 11.7 us -> 14.4 us  [the longest x6 7.65 us: scatter(): lax.ppermute(parts[k], 'space', [(i, (i + k) % count) for i in range(coun...]
    pallas_call x3 -> x6, Pallas kernels: 34.9 us -> 34.7 us  [call(): pl.pallas_call(unpacked, out_shape=out_shapes, in_specs=[pl.BlockSpec(mem...]
    ppermute x6 -> x7, starting transfers between devices: 9.13 us -> 9.1 us  [flip(): lax.ppermute(array, axis, [(i, i ^ bit) for i in range(lax.axis_size(axis...]
  transfers between devices with their start and end apart: 16 -> 23, of which waited for: 8 -> 10; matrix products, arithmetic and copies ran while one was open for 0% -> 0% of each run, Pallas kernels for 5% -> 21%
where the time goes in v2:
time: 101 us; the launch traced here: 99.8 us
  Pallas kernels  42.8 us (42%)
  starting transfers between devices  30.2 us (30%)
  waiting for transfers between devices  22.7 us (22%)
  local copies, waits for them, and re-layouts  1.88 us (2%)
  other arithmetic  1.49 us (1%)
    pallas_call x6, Pallas kernels, call(): pl.pallas_call(unpacked, out_shape=out_shapes, in_specs=[pl.BlockSpec(mem...  34.7 us
    ppermute x6, waiting for transfers between devices, scatter(): lax.ppermute(parts[k], 'space', [(i, (i + k) % count) for i in range(coun...  10.9 us
    ppermute x7, starting transfers between devices, flip(): lax.ppermute(array, axis, [(i, i ^ bit) for i in range(lax.axis_size(axis...  9.1 us
    ppermute x6, starting transfers between devices, scatter(): lax.ppermute(parts[k], 'space', [(i, (i + k) % count) for i in range(coun...  7.65 us
    ppermute x6, waiting for transfers between devices, gather(): lax.ppermute(total, 'space', [(i, (i + k) % count) for i in range(count)])  7.37 us
    ppermute x6, starting transfers between devices, gather(): lax.ppermute(total, 'space', [(i, (i + k) % count) for i in range(count)])  6.76 us
    pallas_call x1, Pallas kernels, dynamics(): pl.pallas_call(path_kernel, out_shape=(jax.ShapeDtypeStruct((cells, 4, sl...  4.81 us
    ppermute x7, waiting for transfers between devices, flip(): lax.ppermute(array, axis, [(i, i ^ bit) for i in range(lax.axis_size(axis...  4.38 us
  transfers between devices with their start and end apart: 23, of which 10 were waited for; matrix products, arithmetic and copies ran while one was open for 0% of the time, Pallas kernels for 21%

profile of v2, /device:TPU:7, one launch (start us, length us, event | category | flops | bytes accessed | tf_op | source)
XLA Modules:
  0.0 99.8 jit_solution(5234682737709423379)
XLA Ops:
  0.6 0.7 compare_convert_fusion
  1.4 0.7 pad_maximum_fusion.2.raw_ref
  2.1 3.3 %collective-permute-start.1 = (f32[2,5,128]{2,1,0:T(8,128)S(1)}, f32[2,5,128]{2,1,0:T(8,128)S(1)}, u32[]{:S(2)}, u32[]{:S(2)}) collective-permute-start(f32[2,5,128]{2,1,0:T(8,128)S(1)} %pad_maximum_fusion.2.raw_ref), channel_id=1, source_target_pairs={{4,0},{8,4},{12,8},{0,12},{5,1},{9,5},{13,9},{1,13},{6,2},{10,6},{... | collective-permute-start | bytes 15368 | tf_op jit(solution)/shard_map/ppermute | solution.py:609
  5.4 1.2 %copy-done = f32[2,4,128,256]{3,2,1,0:T(8,128)S(1)} copy-done((f32[2,4,128,256]{3,2,1,0:T(8,128)S(1)}, f32[2,4,128,256]{3,2,1,0:T(8,128)}, u32[]{:S(2)}) %copy-start) | copy-done | bytes 1048600
  6.6 0.7 copy-done.1
  7.3 1.1 %shard_map.68 = (f32[4,8,32,256]{3,2,1,0:T(8,128)S(1)}, bf16[10,32,256]{2,1,0:T(8,128)(2,1)S(1)}, bf16[10,32,256]{2,1,0:T(8,128)(2,1)S(1)}) custom-call(f32[2,5,128]{2,1,0:T(8,128)S(1)} %pad_maximum_fusion.2.raw_ref, s32[2]{0:T(128)S(1)} %copy-done.1, f32[2,4,128,256]{3,2,1,0:T(8,128)S(1)} %copy-done), custom_call_target="tpu_custom_call" | custom-call | tf_op jit(solution)/shard_map/pallas_call | solution.py:613
  8.4 3.3 %collective-permute-start.3 = (bf16[10,32,256]{2,1,0:T(8,128)(2,1)S(1)}, bf16[10,32,256]{2,1,0:T(8,128)(2,1)S(1)}, u32[]{:S(2)}, u32[]{:S(2)}) collective-permute-start(bf16[10,32,256]{2,1,0:T(8,128)(2,1)S(1)} %get-tuple-element.34), channel_id=1, source_target_pairs={{4,0},{8,4},{12,8},{0,12},{5,1},{9,5},{13,9},{1,13},{6,2},{10,6},{... | collective-permute-start | bytes 491528 | tf_op jit(solution)/shard_map/ppermute | solution.py:619
  11.7 4.8 %shard_map.67 = (f32[2,4,128]{2,1,0:T(4,128)}, bf16[3,6,14,32,128]{4,3,2,1,0:T(8,128)(2,1)S(1)}) custom-call(f32[2,5,128]{2,1,0:T(8,128)S(1)} %pad_maximum_fusion.2.raw_ref, f32[2,5,128]{2,1,0:T(8,128)S(1)} %collective-permute-done.low_ref, f32[2,5,128]{2,1,0:T(8,128)S(1)} %collective-permute-done.1.high_ref), custom_call_target="tpu_custom_call" | custom-call | flops 4000000000 | bytes 4000000 | tf_op jit(solution)/shard_map/pallas_call | solution.py:620
  16.6 2.2 %shard_map.69 = bf16[2,4,128,256]{3,2,1,0:T(8,128)(2,1)S(1)} custom-call(f32[2,5,128]{2,1,0:T(8,128)S(1)} %pad_maximum_fusion.2.raw_ref, bf16[3,6,14,32,128]{4,3,2,1,0:T(8,128)(2,1)S(1)} %get-tuple-element.31.k_ref, f32[4,8,32,256]{3,2,1,0:T(8,128)S(1)} %get-tuple-element.32.state_ref, bf16[10,32,256]{2,1,0:T(8,128)(2,1)S(1)} %collective-permute-done.2.low_ref, ...), custom_call_target="tpu_custom_call" | custom-call | tf_op jit(solution)/shard_map/pallas_call | solution.py:630
  18.8 2.2 %collective-permute-start.4 = (bf16[1024,256]{1,0:T(8,128)(2,1)S(1)}, bf16[1024,256]{1,0:T(8,128)(2,1)S(1)}, u32[]{:S(2)}, u32[]{:S(2)}) collective-permute-start(bf16[1024,256]{1,0:T(8,128)(2,1)S(1)} %bitcast.11), channel_id=1, source_target_pairs={{0,1},{1,0},{2,3},{3,2},{4,5},{5,4},{6,7},{7,6},{8,9},{9,8},{10,11... | collective-permute-start | bytes 1572872 | tf_op jit(solution)/shard_map/ppermute | solution.py:328
  21.2 1.3 %collective-permute-done.4.refs_1_.refs_7_ = bf16[1024,256]{1,0:T(8,128)(2,1)S(1)} collective-permute-done((bf16[1024,256]{1,0:T(8,128)(2,1)S(1)}, bf16[1024,256]{1,0:T(8,128)(2,1)S(1)}, u32[]{:S(2)}, u32[]{:S(2)}) %collective-permute-start.4) | collective-permute-done | bytes 524320 | tf_op jit(solution)/shard_map/ppermute | solution.py:328
  23.2 2.0 %collective-permute-start.5 = (f32[80,256]{1,0:T(8,128)S(1)}, f32[80,256]{1,0:T(8,128)S(1)}, u32[]{:S(2)}, u32[]{:S(2)}) collective-permute-start(f32[80,256]{1,0:T(8,128)S(1)} %get-tuple-element.36), channel_id=1, source_target_pairs={{0,4},{4,8},{8,12},{12,0},{1,5},{5,9},{9,13},{13,1},{2,6},{6,10},{... | collective-permute-start | bytes 245768 | tf_op jit(solution)/shard_map/ppermute | solution.py:342
  25.1 1.5 %collective-permute-start.6 = (f32[80,256]{1,0:T(8,128)S(1)}, f32[80,256]{1,0:T(8,128)S(1)}, u32[]{:S(2)}, u32[]{:S(2)}) collective-permute-start(f32[80,256]{1,0:T(8,128)S(1)} %get-tuple-element.37), channel_id=1, source_target_pairs={{0,8},{4,12},{8,0},{12,4},{1,9},{5,13},{9,1},{13,5},{2,10},{6,14},... | collective-permute-start | bytes 245768 | tf_op jit(solution)/shard_map/ppermute | solution.py:342
  26.6 0.9 collective-permute-start.7
  27.5 1.2 %collective-permute-done.5.refs_1_ = f32[80,256]{1,0:T(8,128)S(1)} collective-permute-done((f32[80,256]{1,0:T(8,128)S(1)}, f32[80,256]{1,0:T(8,128)S(1)}, u32[]{:S(2)}, u32[]{:S(2)}) %collective-permute-start.5) | collective-permute-done | bytes 81952 | tf_op jit(solution)/shard_map/ppermute | solution.py:342
  28.7 4.2 %collective-permute-done.6.refs_2_ = f32[80,256]{1,0:T(8,128)S(1)} collective-permute-done((f32[80,256]{1,0:T(8,128)S(1)}, f32[80,256]{1,0:T(8,128)S(1)}, u32[]{:S(2)}, u32[]{:S(2)}) %collective-permute-start.6) | collective-permute-done | bytes 81952 | tf_op jit(solution)/shard_map/ppermute | solution.py:342
  32.9 1.6 %collective-permute-done.11.refs_1_.refs_8_ = bf16[1024,256]{1,0:T(8,128)(2,1)S(1)} collective-permute-done((bf16[1024,256]{1,0:T(8,128)(2,1)S(1)}, bf16[1024,256]{1,0:T(8,128)(2,1)S(1)}, u32[]{:S(2)}, u32[]{:S(2)}) %collective-permute-start.11) | collective-permute-done | bytes 524320 | tf_op jit(solution)/shard_map/ppermute | solution.py:328
  34.5 0.8 collective-permute-start.12
  35.3 3.1 %collective-permute-start.10 = (f32[80,256]{1,0:T(8,128)S(1)}, f32[80,256]{1,0:T(8,128)S(1)}, u32[]{:S(2)}, u32[]{:S(2)}) collective-permute-start(f32[80,256]{1,0:T(8,128)S(1)} %shard_map.71.refs_3_), channel_id=1, source_target_pairs={{0,12},{4,0},{8,4},{12,8},{1,13},{5,1},{9,5},{13,9},{2,14},{6,2},{... | collective-permute-start | bytes 245768 | tf_op jit(solution)/shard_map/ppermute | solution.py:354
  39.3 1.1 %collective-permute-done.10 = f32[80,256]{1,0:T(8,128)S(1)} collective-permute-done((f32[80,256]{1,0:T(8,128)S(1)}, f32[80,256]{1,0:T(8,128)S(1)}, u32[]{:S(2)}, u32[]{:S(2)}) %collective-permute-start.10) | collective-permute-done | bytes 81952 | tf_op jit(solution)/shard_map/ppermute | solution.py:354
  40.4 6.3 %collective-permute-done.9 = f32[80,256]{1,0:T(8,128)S(1)} collective-permute-done((f32[80,256]{1,0:T(8,128)S(1)}, f32[80,256]{1,0:T(8,128)S(1)}, u32[]{:S(2)}, u32[]{:S(2)}) %collective-permute-start.9) | collective-permute-done | bytes 81952 | tf_op jit(solution)/shard_map/ppermute | solution.py:354
  47.0 0.8 collective-permute-start.16
  47.8 2.4 %collective-permute-start.17 = (f32[128,256]{1,0:T(8,128)S(1)}, f32[128,256]{1,0:T(8,128)S(1)}, u32[]{:S(2)}, u32[]{:S(2)}) collective-permute-start(f32[128,256]{1,0:T(8,128)S(1)} %get-tuple-element.47), channel_id=1, source_target_pairs={{0,12},{4,0},{8,4},{12,8},{1,13},{5,1},{9,5},{13,9},{2,14},{6,2},{... | collective-permute-start | bytes 393224 | tf_op jit(solution)/shard_map/ppermute | solution.py:342
  50.3 2.1 %collective-permute-start.13 = (f32[4,80,256]{2,1,0:T(8,128)S(1)}, f32[4,80,256]{2,1,0:T(8,128)S(1)}, u32[]{:S(2)}, u32[]{:S(2)}) collective-permute-start(f32[4,80,256]{2,1,0:T(8,128)S(1)} %pad_maximum_fusion.1.refs_4_.refs_0_), channel_id=1, source_target_pairs={{0,1},{1,0},{2,3},{3,2},{4,5},{5,4},{6,7},{7,6},{8,9},{9,8},{10,11... | collective-permute-start | bytes 983048 | tf_op jit(solution)/shard_map/ppermute | solution.py:328
  52.4 0.8 collective-permute-done.15.refs_1_
  53.2 4.5 %collective-permute-done.16.refs_2_ = f32[128,256]{1,0:T(8,128)S(1)} collective-permute-done((f32[128,256]{1,0:T(8,128)S(1)}, f32[128,256]{1,0:T(8,128)S(1)}, u32[]{:S(2)}, u32[]{:S(2)}) %collective-permute-start.16) | collective-permute-done | bytes 131104 | tf_op jit(solution)/shard_map/ppermute | solution.py:342
  58.1 2.5 %collective-permute-start.18 = (f32[4,80,256]{2,1,0:T(8,128)S(1)}, f32[4,80,256]{2,1,0:T(8,128)S(1)}, u32[]{:S(2)}, u32[]{:S(2)}) collective-permute-start(f32[4,80,256]{2,1,0:T(8,128)S(1)} %collective-permute-done.14.refs_2_), channel_id=1, source_target_pairs={{0,1},{1,0},{2,3},{3,2},{4,5},{5,4},{6,7},{7,6},{8,9},{9,8},{10,11... | collective-permute-start | bytes 983048 | tf_op jit(solution)/shard_map/ppermute | solution.py:328
  60.6 3.0 %collective-permute-start.21 = (f32[128,256]{1,0:T(8,128)S(1)}, f32[128,256]{1,0:T(8,128)S(1)}, u32[]{:S(2)}, u32[]{:S(2)}) collective-permute-start(f32[128,256]{1,0:T(8,128)S(1)} %shard_map.73), channel_id=1, source_target_pairs={{0,12},{4,0},{8,4},{12,8},{1,13},{5,1},{9,5},{13,9},{2,14},{6,2},{... | collective-permute-start | bytes 393224 | tf_op jit(solution)/shard_map/ppermute | solution.py:354
  63.9 13.5 %shard_map.74 = (f32[512,512]{1,0:T(8,128)S(1)}, f32[1,512]{1,0:T(1,128)S(1)}) custom-call(f32[4,80,256]{2,1,0:T(8,128)S(1)} %pad_maximum_fusion.1.refs_4_.refs_0_, f32[4,80,256]{2,1,0:T(8,128)S(1)} %collective-permute-done.13.refs_1_, f32[4,80,256]{2,1,0:T(8,128)S(1)} %collective-permute-done.14.refs_2_, f32[4,80,256]{2,1,0:T(8,128)S(1)} %collective-permute-done.18.refs_3_), custom_call_target="tpu_custom_call" | custom-call | flops 16000000000 | bytes 4000000 | tf_op jit(solution)/shard_map/pallas_call | solution.py:317
  77.5 0.8 collective-permute-start.22
  78.2 1.5 %collective-permute-done.22.refs_5_ = f32[4,128,256]{2,1,0:T(8,128)S(1)} collective-permute-done((f32[4,128,256]{2,1,0:T(8,128)S(1)}, f32[4,128,256]{2,1,0:T(8,128)S(1)}, u32[]{:S(2)}, u32[]{:S(2)}) %collective-permute-start.22) | collective-permute-done | bytes 524320 | tf_op jit(solution)/shard_map/ppermute | solution.py:328
  79.8 20.0 %shard_map.75 = (f32[1024,256]{1,0:T(8,128)}, f32[1,256]{1,0:T(1,128)}) custom-call(f32[4,80,256]{2,1,0:T(8,128)S(1)} %pad_maximum_fusion.1.refs_4_.refs_0_, f32[4,80,256]{2,1,0:T(8,128)S(1)} %collective-permute-done.13.refs_1_, f32[4,80,256]{2,1,0:T(8,128)S(1)} %collective-permute-done.14.refs_2_, f32[4,80,256]{2,1,0:T(8,128)S(1)} %collective-permute-done.18.refs_3_, ...), custom_call_target="tpu_custom_call" | custom-call | tf_op jit(solution)/shard_map/pallas_call | solution.py:317
  (31 shorter events, 2.9 us)
Async XLA Ops:
  2.1 9.7 %collective-permute-start.1 = (f32[2,5,128]{2,1,0:T(8,128)S(1)}, f32[2,5,128]{2,1,0:T(8,128)S(1)}, u32[]{:S(2)}, u32[]{:S(2)}) collective-permute-start(f32[2,5,128]{2,1,0:T(8,128)S(1)} %pad_maximum_fusion.2.raw_ref), channel_id=1, source_target_pairs={{4,0},{8,4},{12,8},{0,12},{5,1},{9,5},{13,9},{1,13},{6,2},{10,6},{... | collective-permute-start | bytes 15368 | tf_op jit(solution)/shard_map/ppermute | solution.py:609
  5.4 6.4 %collective-permute-start = (f32[2,5,128]{2,1,0:T(8,128)S(1)}, f32[2,5,128]{2,1,0:T(8,128)S(1)}, u32[]{:S(2)}, u32[]{:S(2)}) collective-permute-start(f32[2,5,128]{2,1,0:T(8,128)S(1)} %pad_maximum_fusion.2.raw_ref), channel_id=1, source_target_pairs={{0,4},{4,8},{8,12},{12,0},{1,5},{5,9},{9,13},{13,1},{2,6},{6,10},{... | collective-permute-start | bytes 15368 | tf_op jit(solution)/shard_map/ppermute | solution.py:609
  5.4 1.2 %copy-start = (f32[2,4,128,256]{3,2,1,0:T(8,128)S(1)}, f32[2,4,128,256]{3,2,1,0:T(8,128)}, u32[]{:S(2)}) copy-start(f32[2,4,128,256]{3,2,1,0:T(8,128)} %tangent_ref.1) | copy-start | bytes 3145732
  6.6 0.7 copy-start.1
  8.4 8.2 %collective-permute-start.2 = (bf16[10,32,256]{2,1,0:T(8,128)(2,1)S(1)}, bf16[10,32,256]{2,1,0:T(8,128)(2,1)S(1)}, u32[]{:S(2)}, u32[]{:S(2)}) collective-permute-start(bf16[10,32,256]{2,1,0:T(8,128)(2,1)S(1)} %get-tuple-element.33), channel_id=1, source_target_pairs={{0,4},{4,8},{8,12},{12,0},{1,5},{5,9},{9,13},{13,1},{2,6},{6,10},{... | collective-permute-start | bytes 491528 | tf_op jit(solution)/shard_map/ppermute | solution.py:619
  8.4 8.1 %collective-permute-start.3 = (bf16[10,32,256]{2,1,0:T(8,128)(2,1)S(1)}, bf16[10,32,256]{2,1,0:T(8,128)(2,1)S(1)}, u32[]{:S(2)}, u32[]{:S(2)}) collective-permute-start(bf16[10,32,256]{2,1,0:T(8,128)(2,1)S(1)} %get-tuple-element.34), channel_id=1, source_target_pairs={{4,0},{8,4},{12,8},{0,12},{5,1},{9,5},{13,9},{1,13},{6,2},{10,6},{... | collective-permute-start | bytes 491528 | tf_op jit(solution)/shard_map/ppermute | solution.py:619
  18.8 3.7 %collective-permute-start.4 = (bf16[1024,256]{1,0:T(8,128)(2,1)S(1)}, bf16[1024,256]{1,0:T(8,128)(2,1)S(1)}, u32[]{:S(2)}, u32[]{:S(2)}) collective-permute-start(bf16[1024,256]{1,0:T(8,128)(2,1)S(1)} %bitcast.11), channel_id=1, source_target_pairs={{0,1},{1,0},{2,3},{3,2},{4,5},{5,4},{6,7},{7,6},{8,9},{9,8},{10,11... | collective-permute-start | bytes 1572872 | tf_op jit(solution)/shard_map/ppermute | solution.py:328
  21.0 13.5 %collective-permute-start.11 = (bf16[1024,256]{1,0:T(8,128)(2,1)S(1)}, bf16[1024,256]{1,0:T(8,128)(2,1)S(1)}, u32[]{:S(2)}, u32[]{:S(2)}) collective-permute-start(bf16[1024,256]{1,0:T(8,128)(2,1)S(1)} %bitcast.12), channel_id=1, source_target_pairs={{0,2},{1,3},{2,0},{3,1},{4,6},{5,7},{6,4},{7,5},{8,10},{9,11},{10,... | collective-permute-start | bytes 1572872 | tf_op jit(solution)/shard_map/ppermute | solution.py:328
  23.2 5.5 %collective-permute-start.5 = (f32[80,256]{1,0:T(8,128)S(1)}, f32[80,256]{1,0:T(8,128)S(1)}, u32[]{:S(2)}, u32[]{:S(2)}) collective-permute-start(f32[80,256]{1,0:T(8,128)S(1)} %get-tuple-element.36), channel_id=1, source_target_pairs={{0,4},{4,8},{8,12},{12,0},{1,5},{5,9},{9,13},{13,1},{2,6},{6,10},{... | collective-permute-start | bytes 245768 | tf_op jit(solution)/shard_map/ppermute | solution.py:342
  25.1 7.7 %collective-permute-start.6 = (f32[80,256]{1,0:T(8,128)S(1)}, f32[80,256]{1,0:T(8,128)S(1)}, u32[]{:S(2)}, u32[]{:S(2)}) collective-permute-start(f32[80,256]{1,0:T(8,128)S(1)} %get-tuple-element.37), channel_id=1, source_target_pairs={{0,8},{4,12},{8,0},{12,4},{1,9},{5,13},{9,1},{13,5},{2,10},{6,14},... | collective-permute-start | bytes 245768 | tf_op jit(solution)/shard_map/ppermute | solution.py:342
  26.6 6.3 %collective-permute-start.7 = (f32[80,256]{1,0:T(8,128)S(1)}, f32[80,256]{1,0:T(8,128)S(1)}, u32[]{:S(2)}, u32[]{:S(2)}) collective-permute-start(f32[80,256]{1,0:T(8,128)S(1)} %get-tuple-element.38), channel_id=1, source_target_pairs={{0,12},{4,0},{8,4},{12,8},{1,13},{5,1},{9,5},{13,9},{2,14},{6,2},{... | collective-permute-start | bytes 245768 | tf_op jit(solution)/shard_map/ppermute | solution.py:342
  34.5 4.3 %collective-permute-start.12 = (bf16[1024,256]{1,0:T(8,128)(2,1)S(1)}, bf16[1024,256]{1,0:T(8,128)(2,1)S(1)}, u32[]{:S(2)}, u32[]{:S(2)}) collective-permute-start(bf16[1024,256]{1,0:T(8,128)(2,1)S(1)} %collective-permute-done.11.refs_1_.refs_8_), channel_id=1, source_target_pairs={{0,1},{1,0},{2,3},{3,2},{4,5},{5,4},{6,7},{7,6},{8,9},{9,8},{10,11... | collective-permute-start | bytes 1572872 | tf_op jit(solution)/shard_map/ppermute | solution.py:328
  35.3 5.0 %collective-permute-start.10 = (f32[80,256]{1,0:T(8,128)S(1)}, f32[80,256]{1,0:T(8,128)S(1)}, u32[]{:S(2)}, u32[]{:S(2)}) collective-permute-start(f32[80,256]{1,0:T(8,128)S(1)} %shard_map.71.refs_3_), channel_id=1, source_target_pairs={{0,12},{4,0},{8,4},{12,8},{1,13},{5,1},{9,5},{13,9},{2,14},{6,2},{... | collective-permute-start | bytes 245768 | tf_op jit(solution)/shard_map/ppermute | solution.py:354
  38.4 8.2 %collective-permute-start.9 = (f32[80,256]{1,0:T(8,128)S(1)}, f32[80,256]{1,0:T(8,128)S(1)}, u32[]{:S(2)}, u32[]{:S(2)}) collective-permute-start(f32[80,256]{1,0:T(8,128)S(1)} %shard_map.71.refs_3_), channel_id=1, source_target_pairs={{0,8},{4,12},{8,0},{12,4},{1,9},{5,13},{9,1},{13,5},{2,10},{6,14},... | collective-permute-start | bytes 245768 | tf_op jit(solution)/shard_map/ppermute | solution.py:354
  38.4 8.2 %collective-permute-start.8 = (f32[80,256]{1,0:T(8,128)S(1)}, f32[80,256]{1,0:T(8,128)S(1)}, u32[]{:S(2)}, u32[]{:S(2)}) collective-permute-start(f32[80,256]{1,0:T(8,128)S(1)} %shard_map.71.refs_3_), channel_id=1, source_target_pairs={{0,4},{4,8},{8,12},{12,0},{1,5},{5,9},{9,13},{13,1},{2,6},{6,10},{... | collective-permute-start | bytes 245768 | tf_op jit(solution)/shard_map/ppermute | solution.py:354
  46.7 11.3 %collective-permute-start.14 = (f32[4,80,256]{2,1,0:T(8,128)S(1)}, f32[4,80,256]{2,1,0:T(8,128)S(1)}, u32[]{:S(2)}, u32[]{:S(2)}) collective-permute-start(f32[4,80,256]{2,1,0:T(8,128)S(1)} %pad_maximum_fusion.1.refs_4_.refs_0_), channel_id=1, source_target_pairs={{0,2},{1,3},{2,0},{3,1},{4,6},{5,7},{6,4},{7,5},{8,10},{9,11},{10,... | collective-permute-start | bytes 983048 | tf_op jit(solution)/shard_map/ppermute | solution.py:328
  47.0 6.2 %collective-permute-start.15 = (f32[128,256]{1,0:T(8,128)S(1)}, f32[128,256]{1,0:T(8,128)S(1)}, u32[]{:S(2)}, u32[]{:S(2)}) collective-permute-start(f32[128,256]{1,0:T(8,128)S(1)} %get-tuple-element.45), channel_id=1, source_target_pairs={{0,4},{4,8},{8,12},{12,0},{1,5},{5,9},{9,13},{13,1},{2,6},{6,10},{... | collective-permute-start | bytes 393224 | tf_op jit(solution)/shard_map/ppermute | solution.py:342
  47.0 10.7 %collective-permute-start.16 = (f32[128,256]{1,0:T(8,128)S(1)}, f32[128,256]{1,0:T(8,128)S(1)}, u32[]{:S(2)}, u32[]{:S(2)}) collective-permute-start(f32[128,256]{1,0:T(8,128)S(1)} %get-tuple-element.46), channel_id=1, source_target_pairs={{0,8},{4,12},{8,0},{12,4},{1,9},{5,13},{9,1},{13,5},{2,10},{6,14},... | collective-permute-start | bytes 393224 | tf_op jit(solution)/shard_map/ppermute | solution.py:342
  47.8 10.2 %collective-permute-start.17 = (f32[128,256]{1,0:T(8,128)S(1)}, f32[128,256]{1,0:T(8,128)S(1)}, u32[]{:S(2)}, u32[]{:S(2)}) collective-permute-start(f32[128,256]{1,0:T(8,128)S(1)} %get-tuple-element.47), channel_id=1, source_target_pairs={{0,12},{4,0},{8,4},{12,8},{1,13},{5,1},{9,5},{13,9},{2,14},{6,2},{... | collective-permute-start | bytes 393224 | tf_op jit(solution)/shard_map/ppermute | solution.py:342
  50.3 13.6 %collective-permute-start.13 = (f32[4,80,256]{2,1,0:T(8,128)S(1)}, f32[4,80,256]{2,1,0:T(8,128)S(1)}, u32[]{:S(2)}, u32[]{:S(2)}) collective-permute-start(f32[4,80,256]{2,1,0:T(8,128)S(1)} %pad_maximum_fusion.1.refs_4_.refs_0_), channel_id=1, source_target_pairs={{0,1},{1,0},{2,3},{3,2},{4,5},{5,4},{6,7},{7,6},{8,9},{9,8},{10,11... | collective-permute-start | bytes 983048 | tf_op jit(solution)/shard_map/ppermute | solution.py:328
  58.1 5.9 %collective-permute-start.18 = (f32[4,80,256]{2,1,0:T(8,128)S(1)}, f32[4,80,256]{2,1,0:T(8,128)S(1)}, u32[]{:S(2)}, u32[]{:S(2)}) collective-permute-start(f32[4,80,256]{2,1,0:T(8,128)S(1)} %collective-permute-done.14.refs_2_), channel_id=1, source_target_pairs={{0,1},{1,0},{2,3},{3,2},{4,5},{5,4},{6,7},{7,6},{8,9},{9,8},{10,11... | collective-permute-start | bytes 983048 | tf_op jit(solution)/shard_map/ppermute | solution.py:328
  60.6 16.8 %collective-permute-start.21 = (f32[128,256]{1,0:T(8,128)S(1)}, f32[128,256]{1,0:T(8,128)S(1)}, u32[]{:S(2)}, u32[]{:S(2)}) collective-permute-start(f32[128,256]{1,0:T(8,128)S(1)} %shard_map.73), channel_id=1, source_target_pairs={{0,12},{4,0},{8,4},{12,8},{1,13},{5,1},{9,5},{13,9},{2,14},{6,2},{... | collective-permute-start | bytes 393224 | tf_op jit(solution)/shard_map/ppermute | solution.py:354
  63.6 13.8 %collective-permute-start.20 = (f32[128,256]{1,0:T(8,128)S(1)}, f32[128,256]{1,0:T(8,128)S(1)}, u32[]{:S(2)}, u32[]{:S(2)}) collective-permute-start(f32[128,256]{1,0:T(8,128)S(1)} %shard_map.73), channel_id=1, source_target_pairs={{0,8},{4,12},{8,0},{12,4},{1,9},{5,13},{9,1},{13,5},{2,10},{6,14},... | collective-permute-start | bytes 393224 | tf_op jit(solution)/shard_map/ppermute | solution.py:354
  63.8 13.6 %collective-permute-start.19 = (f32[128,256]{1,0:T(8,128)S(1)}, f32[128,256]{1,0:T(8,128)S(1)}, u32[]{:S(2)}, u32[]{:S(2)}) collective-permute-start(f32[128,256]{1,0:T(8,128)S(1)} %shard_map.73), channel_id=1, source_target_pairs={{0,4},{4,8},{8,12},{12,0},{1,5},{5,9},{9,13},{13,1},{2,6},{6,10},{... | collective-permute-start | bytes 393224 | tf_op jit(solution)/shard_map/ppermute | solution.py:354
  77.5 2.3 %collective-permute-start.22 = (f32[4,128,256]{2,1,0:T(8,128)S(1)}, f32[4,128,256]{2,1,0:T(8,128)S(1)}, u32[]{:S(2)}, u32[]{:S(2)}) collective-permute-start(f32[4,128,256]{2,1,0:T(8,128)S(1)} %pad_maximum_fusion.refs_4_), channel_id=1, source_target_pairs={{0,1},{1,0},{2,3},{3,2},{4,5},{5,4},{6,7},{7,6},{8,9},{9,8},{10,11... | collective-permute-start | bytes 1572872 | tf_op jit(solution)/shard_map/ppermute | solution.py:328

commit v3 on v2

v3 whole, which is shorter than its diff:
```python
import jax
import jax.numpy as jnp
from jax import lax
from jax.experimental import pallas as pl
from jax.experimental.pallas import tpu as pltpu
from jax.sharding import PartitionSpec as P

STEPS = 2


DT = 0.005
CUT2 = 2.0 ** (1.0 / 3.0)
WIDE, TALL, ITEMS = 8, 16, 5


BLOCK = 128
TILE = 8
NEAR = 3
BF16 = jnp.bfloat16
F32 = jnp.float32


def matmul(a, b, dims):
    return lax.dot_general(a, b, (dims, ((), ())), preferred_element_type=F32)


def two_parts(a):
    high = a.astype(BF16)
    return high, (a - high.astype(F32)).astype(BF16)


def three_pass(a, b, axis_a):
    a_high, a_low = two_parts(a)
    b_high, b_low = two_parts(b)
    left = jnp.concatenate([a_high, a_high, a_low], axis=axis_a)
    right = jnp.concatenate([b_high, b_low, b_high], axis=0)
    return matmul(left, right, ((axis_a,), (0,)))


def spread(row, sublane):
    return jnp.broadcast_to(row[sublane : sublane + 1, :], row.shape)


def columns_of(tile, group):
    return [jnp.broadcast_to(tile[:, k : k + 1], tile.shape) for k in range(TILE * group, TILE * (group + 1))]


def factor_block(tiles):
    shape = tiles[0].shape
    sub = lax.broadcasted_iota(jnp.int32, shape, 0)
    lane = lax.broadcasted_iota(jnp.int32, shape, 1)
    tiles, rows_out, pivots = list(tiles), [], []
    cols = columns_of(tiles[0], 0)
    for j, tile in enumerate(tiles):
        first, more = TILE * j, j + 1 < len(tiles)
        if more:
            ahead, cols_next, ahead_next = (
                columns_of(tile, j + 1), columns_of(tiles[j + 1], j), columns_of(tiles[j + 1], j + 1)
            )
        inverse, ratio, rows = [], {}, []
        pivot = jnp.zeros(shape, F32)
        for k in range(TILE):
            top = spread(cols[k], k)
            pivot = jnp.where(sub == k, top, pivot)
            inverse.append(1.0 / top)
            for m in range(k + 1, TILE):
                ratio[k, m] = spread(cols[m], k) * inverse[k]
                cols[m] = cols[m] - cols[k] * ratio[k, m]
            rows.append(spread(tile, k) + jnp.where(lane == first + k, 1.0, 0.0))
            tile = tile - jnp.where(sub > k, cols[k] * inverse[k], 0.0) * rows[k]
            if more:
                for m in range(TILE):
                    part = spread(ahead[m], k) * inverse[k]
                    ahead[m] = ahead[m] - cols[k] * part
                    ahead_next[m] = ahead_next[m] - cols_next[k] * part
                for m in range(k + 1, TILE):
                    cols_next[m] = cols_next[m] - cols_next[k] * ratio[k, m]
                tiles[j + 1] = tiles[j + 1] - (cols_next[k] * inverse[k]) * rows[k]
        root = lax.rsqrt(pivot)
        unit = jnp.where(lane < sub + first, tile, jnp.where(lane == sub + first, 1.0, 0.0)) * root
        rows_out.append(unit)
        near = min(j + 1 + NEAR, len(tiles))
        if near < len(tiles):
            scaled = jnp.where(lane < first + TILE, unit, tile * root)
            high, low = [part.astype(F32) for part in two_parts(scaled)]
            left = jnp.concatenate([high, high, low], axis=0)[:, TILE * near :]
            right = jnp.concatenate([high, low, high], axis=0)
            update = matmul(left.astype(BF16), right.astype(BF16), ((0,), (0,)))
            group = jnp.logical_and(lane >= first, lane < first + TILE)
            for i in range(near, len(tiles)):
                at = TILE * (i - near)
                tiles[i] = jnp.where(group, 0.0, tiles[i]) - update[at : at + TILE, :]
        for i in range(j + 2, near):
            low, below = columns_of(tiles[i], j), tiles[i]
            for k in range(TILE):
                for m in range(k + 1, TILE):
                    low[m] = low[m] - low[k] * ratio[k, m]
                below = below - (low[k] * inverse[k]) * rows[k]
            tiles[i] = below
        pivots.append(pivot)
        if more:
            cols = ahead_next
    return rows_out, pivots


def eliminate(total, work, pivots):
    size = total * BLOCK
    part = [slice(i * BLOCK, (i + 1) * BLOCK) for i in range(total)]
    for step in range(total):
        own, rest = part[step], slice((step + 1) * BLOCK, size)
        top = step * BLOCK
        tiles = [work[top + TILE * i : top + TILE * (i + 1), own] for i in range(BLOCK // TILE)]
        rows_out, pivot_tiles = factor_block(tiles)
        for i in range(BLOCK // TILE):
            pivots[top + TILE * i : top + TILE * (i + 1), :] = pivot_tiles[i]
        inverse = jnp.concatenate(rows_out, axis=0)
        if step + 1 < total:
            after = part[step + 1]
            across = three_pass(inverse, work[own, after], 1)
            work[after, after] = work[after, after] - three_pass(across, across, 0)
            work[own, after] = across
            if step + 2 < total:
                last = slice((step + 2) * BLOCK, size)
                beyond = three_pass(inverse, work[own, last], 1)
                work[own, last] = beyond
                work[after, last] = work[after, last] - three_pass(across, beyond, 0)
                work[last, last] = work[last, last] - three_pass(beyond, beyond, 0)
        if step:
            before = slice(0, top)
            work[own, before] = three_pass(inverse, work[own, before], 1)
            if step + 1 < total:
                work[rest, before] = work[rest, before] - three_pass(work[own, rest], work[own, before], 0)
        work[own, own] = inverse
        if step + 1 < total:
            work[rest, own] = -three_pass(work[own, rest], inverse, 0)


def share_pair(k, me, half, x_own, x_far, out_ref, rows):
    lower = me < (me ^ k)

    @pl.when(lower)
    def _():
        out_ref[rows, :] = matmul(x_own[:, 0:half], x_far[...], ((0,), (0,)))

    @pl.when(jnp.logical_not(lower))
    def _():
        out_ref[rows, :] = matmul(x_far[:, half:], x_own[...], ((0,), (0,)))


def deal(part, out_refs):
    size, pieces = out_refs[0].shape[0], len(out_refs)
    for k in range(pieces):
        start = pl.multiple_of(lax.rem(lax.axis_index("space") + k, pieces) * size, 8)
        out_refs[k][...] = part[pl.ds(start, size), :]


def near_gram_kernel(x_refs, out_refs, part):
    me = lax.axis_index("tangent")
    half = x_refs[0].shape[1] // 2
    quarter = half // 2
    own = x_refs[0][...]
    part[0:half, :] = matmul(own[:, 0:half], own, ((0,), (0,)))
    last = matmul(own[:, half:], own[:, half:], ((0,), (0,)))
    part[half : half + quarter, 0:half] = last[0:quarter]
    part[half : half + quarter, half:] = last[quarter:]
    for k in range(1, len(x_refs)):
        at = half + quarter + (k - 1) * half
        share_pair(k, me, half, x_refs[0], x_refs[k], part, slice(at, at + half))
    deal(part, out_refs)


def far_gram_kernel(x_own, x_refs, out_refs, part):
    bc = x_own[0].shape[1]
    for k in range(len(x_refs)):
        part[k * bc : (k + 1) * bc, :] = matmul(x_refs[k][...], x_own[0][...], ((0,), (0,)))
    deal(part, out_refs)


def sum_kernel(in_refs, out_ref):
    total = in_refs[0][...]
    for ref in in_refs[1:]:
        total = total + ref[...]
    out_ref[...] = total


def collect(g_ref, scale, part):
    pieces = g_ref.shape[0]
    size = part.shape[0] // pieces
    for j in range(pieces):
        start = pl.multiple_of(lax.rem(lax.axis_index("space") + pieces - j, pieces) * size, 8)
        part[pl.ds(start, size), :] = g_ref[j] * scale


def place_pairs(peer, count, offset, part, work):
    bc = part.shape[1]
    half = bc // 2
    for j in range(1, count):
        other = peer ^ j
        low, high = jnp.minimum(peer, other), jnp.maximum(peer, other)
        top = pl.multiple_of(low * bc + jnp.where(peer == high, half, 0), half)
        at = offset + (j - 1) * half
        work[pl.ds(top, half), pl.ds(pl.multiple_of(high * bc, BLOCK), bc)] = part[at : at + half, :]


def near_blocks(peer, part, work):
    bc = part.shape[1]
    half = bc // 2
    quarter = half // 2
    top = pl.multiple_of(peer * bc, BLOCK)
    work[pl.ds(top, half), pl.ds(top, bc)] = part[0:half, :]
    if half % BLOCK:
        full = part[0:half, half:]
        block = jnp.concatenate([part[half : half + quarter, 0:half], part[half : half + quarter, half:]], axis=0)
        work[pl.ds(top + half, half), pl.ds(top, bc)] = jnp.concatenate([full.T, block], axis=1)
    else:
        right = pl.ds(pl.multiple_of(top + half, BLOCK), half)
        work[pl.ds(top + half, quarter), right] = part[half : half + quarter, 0:half]
        work[pl.ds(top + half + quarter, quarter), right] = part[half : half + quarter, half:]
    place_pairs(peer, work.shape[0] // bc, half + quarter, part, work)


def log_rows(pivots, log_ref):
    eye = lax.broadcasted_iota(jnp.int32, (BLOCK, BLOCK), 0) == lax.broadcasted_iota(jnp.int32, (BLOCK, BLOCK), 1)
    for a in range(pivots.shape[0] // BLOCK):
        block = pivots[a * BLOCK : (a + 1) * BLOCK, :]
        log_ref[:, a * BLOCK : (a + 1) * BLOCK] = 0.5 * jnp.log(
            jnp.sum(jnp.where(eye, block, 0.0), axis=0, keepdims=True)
        )


def lower_blocks(matrix):
    row_block = lax.broadcasted_iota(jnp.int32, matrix.shape, 0) // BLOCK
    col_block = lax.broadcasted_iota(jnp.int32, matrix.shape, 1) // BLOCK
    return jnp.where(row_block >= col_block, matrix, 0.0)


def first_kernel(scale, g_refs, inverse_ref, log_ref, pivots, part):
    me = lax.axis_index("tangent")
    inner = len(g_refs) // 2
    for k in range(2 * inner):

        @pl.when((me < inner) == (k < inner))
        def _():
            collect(g_refs[k], scale, part)
            near_blocks((me ^ k) & (inner - 1), part, inverse_ref)

    eliminate(inverse_ref.shape[0] // BLOCK, inverse_ref, pivots)
    inverse_ref[...] = lower_blocks(inverse_ref[...])
    log_rows(pivots, log_ref)


def second_kernel(
    scale, near_refs, far_refs, x_refs, first_ref, first_log, out_ref, log_ref,
    work, cross, mine, logs, pivots, near_part, far_part,
):
    me = lax.axis_index("tangent")
    shards = len(x_refs)
    inner = shards // 2
    bc = out_ref.shape[1]
    full = work.shape[0]
    top = pl.multiple_of((me & (inner - 1)) * bc, BLOCK)
    rows = pl.ds(top, bc)

    @pl.when(me < inner)
    def _():
        mine[:, 0:full] = first_ref[rows, :]
        mine[:, full:] = jnp.zeros((bc, full), F32)
        log_ref[...] = first_log[:, rows]

    @pl.when(me >= inner)
    def _():
        for k in range(inner):
            collect(far_refs[k], scale, far_part)
            cols = pl.ds(pl.multiple_of((me ^ k) * bc - full, BLOCK), bc)
            for j in range(inner):
                place = pl.ds(pl.multiple_of((me ^ k ^ (j + inner)) * bc, BLOCK), bc)
                cross[place, cols] = far_part[j * bc : (j + 1) * bc, :]
            collect(near_refs[k], scale, near_part)
            near_blocks((me ^ k) & (inner - 1), near_part, work)
        cross[...] = three_pass(first_ref[...], cross[...], 1)
        work[...] = work[...] - three_pass(cross[...], cross[...], 0)
        eliminate(full // BLOCK, work, pivots)
        log_rows(pivots, logs)
        row_block = (lax.broadcasted_iota(jnp.int32, (bc, full), 0) + top) // BLOCK
        col_block = lax.broadcasted_iota(jnp.int32, (bc, full), 1) // BLOCK
        own = jnp.where(row_block >= col_block, work[rows, :], 0.0)
        mine[:, full:] = own
        mine[:, 0:full] = -three_pass(three_pass(own, cross[...].T, 1), first_ref[...], 1)
        log_ref[...] = logs[:, rows]

    def times(x_ref, peer):
        high, low = two_parts(mine[:, pl.ds(pl.multiple_of(peer * bc, BLOCK), bc)])
        return matmul(x_ref[...], high, ((1,), (1,))) + matmul(x_ref[...], low, ((1,), (1,)))

    out_ref[...] = times(x_refs[0], me)
    for k in range(1, shards):
        peer = me ^ k

        @pl.when(peer < me)
        def _():
            out_ref[...] += times(x_refs[k], peer)


def call(kernel, counts, out_shapes, scratch, operands, cost=None, after=()):
    inputs, waits = len(operands), len(after)

    def unpacked(*refs):
        refs = refs[:inputs] + refs[inputs + waits :]
        groups, at = [], 0
        for count in counts:
            groups.append(refs[at : at + count])
            at += count
        kernel(*groups, *refs[at:])

    return pl.pallas_call(
        unpacked,
        out_shape=out_shapes,
        in_specs=[pl.BlockSpec(memory_space=pltpu.VMEM)] * inputs + [pl.BlockSpec(memory_space=pl.ANY)] * waits,
        scratch_shapes=scratch,
        cost_estimate=cost,
        compiler_params=pltpu.CompilerParams(vmem_limit_bytes=48 * 1024 * 1024),
    )(*operands, *after)


def flip(array, axis, bit):
    return lax.ppermute(array, axis, [(i, i ^ bit) for i in range(lax.axis_size(axis))])


def flips(blocks, bits):
    for bit in bits:
        blocks = {**blocks, **{k ^ bit: flip(v, "tangent", bit) for k, v in blocks.items()}}
    return blocks


def around_space(arrays):
    count = lax.axis_size("space")
    return [lax.ppermute(v, "space", [(i, (i + k) % count) for i in range(count)]) for k, v in enumerate(arrays, 1)]


def added(arrived, after=()):
    shape = jax.ShapeDtypeStruct(arrived[0].shape, F32)
    return call(sum_kernel, (len(arrived),), shape, [], arrived, after=after)


def orthonormalize(x):
    shards, count = lax.axis_size("tangent"), lax.axis_size("space")
    rows, bc = x.shape
    half, inner = bc // 2, shards // 2
    direct = count <= 8
    cuts = count if direct else 1
    bits = [1 << b for b in reversed(range(inner.bit_length() - 1))]
    scale = 1.0 / (float(rows) * count)
    near_rows, far_rows = half + half // 2 + (inner - 1) * half, inner * bc

    def dealt(held):
        return (jax.ShapeDtypeStruct((held // cuts, bc), F32),) * cuts

    def spread_out(parts):
        if not direct:
            return [lax.psum(parts[0], "space")]
        return [parts[0]] + around_space(parts[1:])

    far_own = flip(x, "tangent", inner)
    near_x = flips({0: x}, bits)
    near_x = [near_x[k] for k in range(inner)]
    near = call(near_gram_kernel, (inner, cuts), dealt(near_rows), [pltpu.VMEM((near_rows, bc), F32)], near_x)
    near_sum = added(spread_out(near))
    around = [near_sum] + around_space([near_sum] * (cuts - 1))
    far_x = flips({0: lax.optimization_barrier((far_own, near_sum))[0]}, bits)
    far_x = [far_x[k] for k in range(inner)]
    far = call(far_gram_kernel, (1, inner, cuts), dealt(far_rows), [pltpu.VMEM((far_rows, bc), F32)], [x] + far_x)
    arrived = spread_out(far)
    near = jnp.stack(lax.optimization_barrier((around, far[0]))[0])
    far_sum = added(arrived, after=[near])
    far_around = [far_sum] + around_space([far_sum] * (cuts - 1))
    near = flips({0: near}, [inner])
    near[inner] = lax.optimization_barrier((near[inner], far_sum))[0]
    near = flips(near, bits)
    near = [near[k] for k in range(shards)]
    full = inner * bc
    square, column = pltpu.VMEM((full, full), F32), pltpu.VMEM((full, BLOCK), F32)
    near_part = pltpu.VMEM((near_rows, bc), F32)
    first, first_log = call(
        lambda *refs: first_kernel(scale, *refs),
        (shards,),
        (jax.ShapeDtypeStruct((full, full), F32), jax.ShapeDtypeStruct((1, full), F32)),
        [column, near_part],
        near,
        cost=pl.CostEstimate(flops=16 * 10**9, bytes_accessed=4 * 10**6, transcendentals=0),
    )
    far_around = lax.optimization_barrier((far_around, first_log))[0]
    late = flips({0: jnp.stack(far_around)}, bits)
    late = [late[k] for k in range(inner)]
    out, logs = call(
        lambda *refs: second_kernel(scale, *refs),
        (inner, inner, shards),
        (jax.ShapeDtypeStruct((rows, bc), F32), jax.ShapeDtypeStruct((1, bc), F32)),
        [
            square, square, pltpu.VMEM((bc, 2 * full), F32), pltpu.VMEM((1, full), F32),
            column, near_part, pltpu.VMEM((far_rows, bc), F32),
        ],
        near[:inner] + late + near_x + far_x + [first, first_log],
    )
    return out, logs[0]


def site_rows(x, y, tall):
    column = jnp.concatenate([row.astype(jnp.int32) for row in x], axis=1)
    row = jnp.concatenate([v.astype(jnp.int32) + c * TALL for c, v in enumerate(y)], axis=1)
    return column, row


def one_hot(rows, index):
    return jnp.where(lax.broadcasted_iota(jnp.int32, (rows, index.shape[1]), 0) == index, 1.0, 0.0)


def own_sites(position_ref):
    cells = position_ref.shape[0]
    x, y = [[position_ref[c, i : i + 1, :] for c in range(cells)] for i in range(2)]
    return site_rows(x, y, cells * TALL)


def placement(position_ref):
    tall = position_ref.shape[0] * TALL
    column, row = own_sites(position_ref)
    return one_hot(WIDE * tall, column * tall + row).astype(BF16)


def three_parts(a):
    high, rest = a.astype(BF16), None
    rest = a - high.astype(F32)
    mid = rest.astype(BF16)
    return high, mid, (rest - mid.astype(F32)).astype(BF16)


def sort_kernel(position_ref, momentum_ref, count_ref, tangent_ref, state_ref, left_ref, right_ref, raw):
    cells, comps, slots, bc = tangent_ref.shape
    high = cells * TALL
    place = placement(position_ref)
    raw[...] = jnp.zeros(raw.shape, F32)
    lane = lax.broadcasted_iota(jnp.int32, (1, slots), 1)
    for c in range(cells):
        alive = jnp.where(lane < count_ref[c], 1.0, 0.0)
        rows = [position_ref[c, 0:1, :], position_ref[c, 1:2, :], momentum_ref[c, 0:1, :], momentum_ref[c, 1:2, :], alive]
        for item, row in enumerate(rows):
            for p, part in enumerate(three_parts(row)):
                at = ITEMS * (p * cells + c) + item
                raw[at : at + 1, :] = part.astype(F32)
    for ref in (left_ref, right_ref):
        ref[10] = jnp.zeros((high, bc), BF16)
        ref[10, :, 0:slots] = raw[...].astype(BF16)
    slot = lax.broadcasted_iota(jnp.int32, (slots, bc), 0)
    for comp in range(comps):
        rows = [jnp.where(slot < count_ref[c], tangent_ref[c, comp], 0.0) for c in range(cells)]
        top, low = two_parts(jnp.concatenate(rows, axis=0))
        moved = matmul(place, top, ((1,), (0,))) + matmul(place, low, ((1,), (0,)))
        state_ref[comp] = moved.reshape(WIDE, high, bc)
        near = moved.astype(BF16).reshape(WIDE, high, bc)
        if comp < 2:
            left_ref[3 * comp : 3 * comp + 3] = near[0:3]
            right_ref[3 * comp : 3 * comp + 3] = near[WIDE - 3 :]
        else:
            at = 6 + 2 * (comp - 2)
            left_ref[at : at + 2] = near[0:2]
            right_ref[at : at + 2] = near[WIDE - 2 :]


def bond(far_x, far_y, own_x, own_y, both, shift_x, shift_y):
    dx = shift_x + far_x - own_x
    dy = shift_y + far_y - own_y
    dist2 = dx * dx + dy * dy
    within = jnp.logical_and(dist2 < CUT2, both > 0.5)
    weight = jnp.where(within, 1.0, 0.0)
    safe = jnp.where(within, dist2, CUT2)
    inverse = 1.0 / safe
    inv_three = inverse * inverse * inverse
    inv_six = inv_three * inv_three
    energy = 4.0 * (inv_six - inv_three) + 1.0
    energy_1 = 4.0 * (3.0 * inv_three - 6.0 * inv_six) * inverse
    energy_2 = 4.0 * (42.0 * inv_six - 12.0 * inv_three) * inverse * inverse
    taper = 1.0 - safe * (1.0 / CUT2)
    switch = taper * taper
    switch_1 = taper * (-2.0 / CUT2)
    switch_2 = 2.0 / (CUT2 * CUT2)
    twice_1 = (energy_1 * switch + energy * switch_1) * weight * 2.0
    four_2 = (energy_2 * switch + 2.0 * energy_1 * switch_1 + energy * switch_2) * weight * 4.0
    k_xx = twice_1 + four_2 * dx * dx
    k_xy = four_2 * dx * dy
    k_yy = twice_1 + four_2 * dy * dy
    return twice_1 * dx, twice_1 * dy, (k_xx, k_xy, k_yy)


def up(a):
    return pltpu.roll(a, a.shape[0] - 1, 0)


def down(a):
    return pltpu.roll(a, 1, 0)


KICKS = tuple((0.5 if step in (0, STEPS) else 1.0) * DT for step in range(STEPS + 1))


def on_lattice(cells, tall, rows, offset):
    x, y = [[sum(part[c] for part in rows[i]) for c in range(cells)] for i in range(2)]
    column, row = site_rows(x, y, tall)
    stands = one_hot(tall, row)
    flat = [jnp.concatenate(part, axis=1) for item in rows for part in item]
    left = jnp.concatenate([stands * v for v in flat], axis=0).astype(BF16)
    spread_values = matmul(left, one_hot(BLOCK, column + offset).astype(BF16), ((1,), (1,)))
    out, at = [], 0
    for item in rows:
        parts = [spread_values[(at + p) * tall : (at + p + 1) * tall] for p in range(len(item))]
        out.append(sum(parts[1:], parts[0]))
        at += len(item)
    return out


def motion_kernel(
    position_ref, momentum_ref, count_ref, state_ref, low_ref, high_ref, phase_ref, x_ref, wide, bonds
):
    cells, comps, slots, bc = x_ref.shape
    tall = cells * TALL
    halo = STEPS + 1
    columns = WIDE + 2 * halo
    for comp in range(comps):
        wide[comp, halo : halo + WIDE] = state_ref[comp]
        if comp < 2:
            wide[comp, 0:halo] = low_ref[3 * comp : 3 * comp + 3].astype(F32)
            wide[comp, halo + WIDE :] = high_ref[3 * comp : 3 * comp + 3].astype(F32)
        else:
            at = 6 + 2 * (comp - 2)
            wide[comp, 1:halo] = low_ref[at : at + 2].astype(F32)
            wide[comp, halo + WIDE : columns - 1] = high_ref[at : at + 2].astype(F32)
    slot = lax.broadcasted_iota(jnp.int32, (1, slots), 1)
    own = [
        [[part.astype(F32) for part in three_parts(ref[c, i : i + 1, :])] for c in range(cells)]
        for ref in (position_ref, momentum_ref)
        for i in range(2)
    ]
    own = [[[cell[p] for cell in item] for p in range(3)] for item in own]
    own.append([[jnp.where(slot < count_ref[c], 1.0, 0.0) for c in range(cells)]])
    slabs = [on_lattice(cells, tall, own, halo)]
    for ref, offset in ((low_ref, halo - WIDE), (high_ref, halo + WIDE)):
        sent = ref[10, :, 0:slots].astype(F32)

        def row(item, p, c):
            at = ITEMS * (p * cells + c) + item
            return sent[at : at + 1, :]

        rows = [[[row(i, p, c) for c in range(cells)] for p in range(3 if i < 4 else 1)] for i in range(ITEMS)]
        slabs.append(on_lattice(cells, tall, rows, offset))
    x, y, speed_x, speed_y, alive = [a + b + c for a, b, c in zip(*slabs)]
    site = lax.broadcasted_iota(jnp.int32, (tall, BLOCK), 0)
    lane = lax.broadcasted_iota(jnp.int32, (tall, BLOCK), 1)
    shift_y = jnp.where(lax.rem(site, TALL) == TALL - 1, float(TALL), 0.0)
    shift_x = jnp.where(jnp.logical_or(lane == halo - 1, lane == halo + WIDE - 1), float(WIDE), 0.0)

    def right(a):
        return pltpu.roll(a, BLOCK - 1, 1)

    def left(a):
        return pltpu.roll(a, 1, 1)

    beside, over = alive * right(alive), alive * up(alive)
    for step, kick in enumerate(KICKS):
        side_x, side_y, k_side = bond(right(x), right(y), x, y, beside, shift_x, 0.0)
        over_x, over_y, k_over = bond(up(x), up(y), x, y, over, 0.0, shift_y)
        for a, k in enumerate(k_side + k_over):
            bonds[step, a] = k.astype(BF16).astype(F32)
        speed_x = speed_x + kick * (side_x - left(side_x) + over_x - down(over_x))
        speed_y = speed_y + kick * (side_y - left(side_y) + over_y - down(over_y))
        if step < STEPS:
            x, y = x + DT * speed_x, y + DT * speed_y
    column, row = own_sites(position_ref)
    picks = one_hot(BLOCK, column + halo).astype(BF16)
    stands = one_hot(tall, row)
    for item, value in enumerate((x, y, speed_x, speed_y)):
        back = sum(matmul(part, picks, ((1,), (0,))) for part in three_parts(value))
        back = jnp.sum(jnp.where(stands > 0.5, back, 0.0), axis=0, keepdims=True)
        for c in range(cells):
            phase_ref[c, item : item + 1, :] = back[:, c * slots : (c + 1) * slots]

    def rounded(comp, c):
        return wide[comp, c].astype(BF16).astype(F32)

    for step, kick in enumerate(KICKS):

        def push(c, k0, e_x, e_y):
            k_xx, k_xy, k_yy = [
                jnp.broadcast_to(bonds[step, k0 + a][:, c : c + 1], (tall, bc)) for a in range(3)
            ]
            return k_xx * e_x + k_xy * e_y, k_xy * e_x + k_yy * e_y

        low_x, low_y = rounded(0, step), rounded(1, step)
        next_x, next_y = rounded(0, step + 1), rounded(1, step + 1)
        pull_x, pull_y = push(step, 0, next_x - low_x, next_y - low_y)
        for c in range(step + 1, columns - 1 - step):
            low_x, low_y = next_x, next_y
            next_x, next_y = rounded(0, c + 1), rounded(1, c + 1)
            side_x, side_y = push(c, 0, next_x - low_x, next_y - low_y)
            over_x, over_y = push(c, 3, up(low_x) - low_x, up(low_y) - low_y)
            rate_x = wide[2, c] + kick * (side_x - pull_x + over_x - down(over_x))
            rate_y = wide[3, c] + kick * (side_y - pull_y + over_y - down(over_y))
            wide[2, c], wide[3, c] = rate_x, rate_y
            if step < STEPS:
                wide[0, c] = wide[0, c] + DT * rate_x
                wide[1, c] = wide[1, c] + DT * rate_y
            pull_x, pull_y = side_x, side_y
    place = placement(position_ref)
    for comp in range(comps):
        value = wide[comp, halo : halo + WIDE].reshape(WIDE * tall, bc).astype(BF16)
        back = matmul(place, value, ((0,), (0,))).astype(BF16)
        for c in range(cells):
            x_ref[c, comp] = back[c * slots : (c + 1) * slots]


def dynamics(positions, momenta, cell_count, tangent):
    cells, comps, slots, bc = tangent.shape
    tall = cells * TALL
    columns = WIDE + 2 * (STEPS + 1)
    count = lax.axis_size("space")
    forward = [(i, (i + 1) % count) for i in range(count)]
    backward = [(b, a) for a, b in forward]
    halo = jax.ShapeDtypeStruct((11, tall, bc), BF16)
    vmem, smem = pl.BlockSpec(memory_space=pltpu.VMEM), pl.BlockSpec(memory_space=pltpu.SMEM)
    params = pltpu.CompilerParams(vmem_limit_bytes=48 * 1024 * 1024)
    state, left, right = pl.pallas_call(
        sort_kernel,
        out_shape=(jax.ShapeDtypeStruct((comps, WIDE, tall, bc), F32), halo, halo),
        in_specs=[vmem, vmem, smem, vmem],
        scratch_shapes=[pltpu.VMEM((tall, slots), F32)],
        compiler_params=params,
    )(positions, momenta, cell_count, tangent)
    low, high = lax.ppermute(right, "space", forward), lax.ppermute(left, "space", backward)
    return pl.pallas_call(
        motion_kernel,
        out_shape=(jax.ShapeDtypeStruct((cells, 4, slots), F32), jax.ShapeDtypeStruct(tangent.shape, BF16)),
        in_specs=[vmem, vmem, smem, vmem, vmem, vmem],
        scratch_shapes=[
            pltpu.VMEM((comps, columns, tall, bc), F32),
            pltpu.VMEM((STEPS + 1, 6, tall, BLOCK), F32),
        ],
        compiler_params=params,
    )(positions, momenta, cell_count, state, low, high)


def body(positions, momenta, cell_count, tangent):
    phase, x = dynamics(positions, momenta, cell_count, tangent)
    out, stretch = orthonormalize(x.reshape(-1, x.shape[3]))
    return (phase, out.reshape(x.shape), stretch)


def solution(mesh):
    placed = (
        P(("groups", "space"), None, None),
        P(("groups", "space"), None, None),
        P(("groups", "space")),
        P(("groups", "space"), None, None, "tangent"),
    )
    return jax.shard_map(
        body,
        mesh=mesh,
        in_specs=placed,
        out_specs=(
            P(("groups", "space"), None, None),
            P(("groups", "space"), None, None, "tangent"),
            P(("groups", "tangent")),
        ),
        check_vma=False,
    )
```

time: 101 us -> 98.7 us (0.977)
  waiting for transfers between devices: 22.7 us -> 31.3 us
  starting transfers between devices: 30.2 us -> 23.9 us
  Pallas kernels: 42.8 us -> 38 us
  other arithmetic: 1.49 us -> 0.06 us
  local copies, waits for them, and re-layouts: 1.88 us -> 3.23 us
    ppermute x14 -> x12, starting transfers between devices: 17.7 us -> 12.5 us  [around_space(): lax.ppermute(v, 'space', [(i, (i + k) % count) for i in range(count)])]
    ppermute x1, waiting for transfers between devices: 0.01 us -> 4.01 us  [dynamics(): lax.ppermute(right, 'space', forward)]
    ppermute x1, waiting for transfers between devices: 0.01 us -> 3.61 us  [dynamics(): lax.ppermute(left, 'space', backward)]
    pallas_call x2 -> x1, Pallas kernels: 7.02 us -> 3.48 us  [dynamics(): pl.pallas_call(motion_kernel, out_shape=(jax.ShapeDtypeStruct((cells, 4,...]
    unnamed x4 -> x8, local copies, waits for them, and re-layouts: 1.88 us -> 3.23 us
    ppermute x1, starting transfers between devices: 0.06 us -> 1.35 us  [dynamics(): lax.ppermute(right, 'space', forward)]
    pallas_call x6, Pallas kernels: 34.7 us -> 33.4 us  [call(): pl.pallas_call(unpacked, out_shape=out_shapes, in_specs=[pl.BlockSpec(mem...]
    ppermute x1, starting transfers between devices: 3.31 us -> 2.09 us  [dynamics(): lax.ppermute(left, 'space', backward)]
  transfers between devices with their start and end apart: 23 -> 21, of which waited for: 10 -> 12; matrix products, arithmetic and copies ran while one was open for 0% -> 0% of each run, Pallas kernels for 21% -> 15%
where the time goes in v3:
time: 98.7 us; the launch traced here: 97.2 us
  Pallas kernels  38 us (39%)
  waiting for transfers between devices  31.3 us (32%)
  starting transfers between devices  23.9 us (24%)
  local copies, waits for them, and re-layouts  3.23 us (3%)
    pallas_call x6, Pallas kernels, call(): pl.pallas_call(unpacked, out_shape=out_shapes, in_specs=[pl.BlockSpec(mem...  33.4 us
    ppermute x12, waiting for transfers between devices, around_space(): lax.ppermute(v, 'space', [(i, (i + k) % count) for i in range(count)])  19.1 us
    ppermute x12, starting transfers between devices, around_space(): lax.ppermute(v, 'space', [(i, (i + k) % count) for i in range(count)])  12.5 us
    ppermute x7, starting transfers between devices, flip(): lax.ppermute(array, axis, [(i, i ^ bit) for i in range(lax.axis_size(axis...  7.95 us
    ppermute x7, waiting for transfers between devices, flip(): lax.ppermute(array, axis, [(i, i ^ bit) for i in range(lax.axis_size(axis...  4.52 us
    ppermute x1, waiting for transfers between devices, dynamics(): lax.ppermute(right, 'space', forward)  4.01 us
    ppermute x1, waiting for transfers between devices, dynamics(): lax.ppermute(left, 'space', backward)  3.61 us
    pallas_call x1, Pallas kernels, dynamics(): pl.pallas_call(motion_kernel, out_shape=(jax.ShapeDtypeStruct((cells, 4,...  3.48 us
  transfers between devices with their start and end apart: 21, of which 12 were waited for; matrix products, arithmetic and copies ran while one was open for 0% of the time, Pallas kernels for 15%

profile of v3, /device:TPU:7, one launch (start us, length us, event | category | flops | bytes accessed | tf_op | source)
XLA Modules:
  0.0 97.2 jit_solution(9641147366692853112)
XLA Ops:
  0.6 1.2 %copy-done = f32[2,4,128,256]{3,2,1,0:T(8,128)S(1)} copy-done((f32[2,4,128,256]{3,2,1,0:T(8,128)S(1)}, f32[2,4,128,256]{3,2,1,0:T(8,128)}, u32[]{:S(2)}) %copy-start) | copy-done | bytes 1048600
  1.9 0.7 copy-done.1
  2.5 0.7 copy-done.2
  3.9 1.1 %shard_map.67 = (f32[4,8,32,256]{3,2,1,0:T(8,128)S(1)}, bf16[11,32,256]{2,1,0:T(8,128)(2,1)S(1)}, bf16[11,32,256]{2,1,0:T(8,128)(2,1)S(1)}) custom-call(f32[2,2,128]{2,1,0:T(2,128)S(1)} %copy-done.1, f32[2,2,128]{2,1,0:T(2,128)S(1)} %copy-done.2, s32[2]{0:T(128)S(1)} %copy-done.3, f32[2,4,128,256]{3,2,1,0:T(8,128)S(1)} %copy-done), custom_call_target="tpu_custom_call" | custom-call | tf_op jit(solution)/shard_map/pallas_call | solution.py:628
  5.0 1.4 %collective-permute-start = (bf16[11,32,256]{2,1,0:T(8,128)(2,1)S(1)}, bf16[11,32,256]{2,1,0:T(8,128)(2,1)S(1)}, u32[]{:S(2)}, u32[]{:S(2)}) collective-permute-start(bf16[11,32,256]{2,1,0:T(8,128)(2,1)S(1)} %get-tuple-element.31), channel_id=1, source_target_pairs={{0,4},{4,8},{8,12},{12,0},{1,5},{5,9},{9,13},{13,1},{2,6},{6,10},{... | collective-permute-start | bytes 540680 | tf_op jit(solution)/shard_map/ppermute | solution.py:635
  6.3 2.1 %collective-permute-start.1 = (bf16[11,32,256]{2,1,0:T(8,128)(2,1)S(1)}, bf16[11,32,256]{2,1,0:T(8,128)(2,1)S(1)}, u32[]{:S(2)}, u32[]{:S(2)}) collective-permute-start(bf16[11,32,256]{2,1,0:T(8,128)(2,1)S(1)} %get-tuple-element.32), channel_id=1, source_target_pairs={{4,0},{8,4},{12,8},{0,12},{5,1},{9,5},{13,9},{1,13},{6,2},{10,6},{... | collective-permute-start | bytes 540680 | tf_op jit(solution)/shard_map/ppermute | solution.py:635
  8.4 4.0 %collective-permute-done.low_ref = bf16[11,32,256]{2,1,0:T(8,128)(2,1)S(1)} collective-permute-done((bf16[11,32,256]{2,1,0:T(8,128)(2,1)S(1)}, bf16[11,32,256]{2,1,0:T(8,128)(2,1)S(1)}, u32[]{:S(2)}, u32[]{:S(2)}) %collective-permute-start) | collective-permute-done | bytes 180256 | tf_op jit(solution)/shard_map/ppermute | solution.py:635
  12.4 3.6 %collective-permute-done.1.high_ref = bf16[11,32,256]{2,1,0:T(8,128)(2,1)S(1)} collective-permute-done((bf16[11,32,256]{2,1,0:T(8,128)(2,1)S(1)}, bf16[11,32,256]{2,1,0:T(8,128)(2,1)S(1)}, u32[]{:S(2)}, u32[]{:S(2)}) %collective-permute-start.1) | collective-permute-done | bytes 180256 | tf_op jit(solution)/shard_map/ppermute | solution.py:635
  16.0 3.5 %shard_map.68 = (f32[2,4,128]{2,1,0:T(4,128)}, bf16[2,4,128,256]{3,2,1,0:T(8,128)(2,1)S(1)}) custom-call(f32[2,2,128]{2,1,0:T(2,128)S(1)} %copy-done.1, f32[2,2,128]{2,1,0:T(2,128)S(1)} %copy-done.2, s32[2]{0:T(128)S(1)} %copy-done.3, f32[4,8,32,256]{3,2,1,0:T(8,128)S(1)} %get-tuple-element.30.state_ref, ...), custom_call_target="tpu_custom_call" | custom-call | tf_op jit(solution)/shard_map/pallas_call | solution.py:636
  19.5 1.1 %collective-permute-start.2 = (bf16[1024,256]{1,0:T(8,128)(2,1)S(1)}, bf16[1024,256]{1,0:T(8,128)(2,1)S(1)}, u32[]{:S(2)}, u32[]{:S(2)}) collective-permute-start(bf16[1024,256]{1,0:T(8,128)(2,1)S(1)} %bitcast.11), channel_id=1, source_target_pairs={{0,1},{1,0},{2,3},{3,2},{4,5},{5,4},{6,7},{7,6},{8,9},{9,8},{10,11... | collective-permute-start | bytes 1572872 | tf_op jit(solution)/shard_map/ppermute | solution.py:326
  20.9 1.3 %collective-permute-done.2.refs_1_.refs_5_ = bf16[1024,256]{1,0:T(8,128)(2,1)S(1)} collective-permute-done((bf16[1024,256]{1,0:T(8,128)(2,1)S(1)}, bf16[1024,256]{1,0:T(8,128)(2,1)S(1)}, u32[]{:S(2)}, u32[]{:S(2)}) %collective-permute-start.2) | collective-permute-done | bytes 524320 | tf_op jit(solution)/shard_map/ppermute | solution.py:326
  22.8 0.9 collective-permute-start.3
  23.7 1.5 %collective-permute-start.4 = (f32[80,256]{1,0:T(8,128)S(1)}, f32[80,256]{1,0:T(8,128)S(1)}, u32[]{:S(2)}, u32[]{:S(2)}) collective-permute-start(f32[80,256]{1,0:T(8,128)S(1)} %get-tuple-element.37), channel_id=1, source_target_pairs={{0,8},{4,12},{8,0},{12,4},{1,9},{5,13},{9,1},{13,5},{2,10},{6,14},... | collective-permute-start | bytes 245768 | tf_op jit(solution)/shard_map/ppermute | solution.py:337
  25.2 1.1 %collective-permute-start.5 = (f32[80,256]{1,0:T(8,128)S(1)}, f32[80,256]{1,0:T(8,128)S(1)}, u32[]{:S(2)}, u32[]{:S(2)}) collective-permute-start(f32[80,256]{1,0:T(8,128)S(1)} %get-tuple-element.38), channel_id=1, source_target_pairs={{0,12},{4,0},{8,4},{12,8},{1,13},{5,1},{9,5},{13,9},{2,14},{6,2},{... | collective-permute-start | bytes 245768 | tf_op jit(solution)/shard_map/ppermute | solution.py:337
  26.3 2.1 %collective-permute-done.3.refs_1_ = f32[80,256]{1,0:T(8,128)S(1)} collective-permute-done((f32[80,256]{1,0:T(8,128)S(1)}, f32[80,256]{1,0:T(8,128)S(1)}, u32[]{:S(2)}, u32[]{:S(2)}) %collective-permute-start.3) | collective-permute-done | bytes 81952 | tf_op jit(solution)/shard_map/ppermute | solution.py:337
  28.4 4.1 %collective-permute-done.4.refs_2_ = f32[80,256]{1,0:T(8,128)S(1)} collective-permute-done((f32[80,256]{1,0:T(8,128)S(1)}, f32[80,256]{1,0:T(8,128)S(1)}, u32[]{:S(2)}, u32[]{:S(2)}) %collective-permute-start.4) | collective-permute-done | bytes 81952 | tf_op jit(solution)/shard_map/ppermute | solution.py:337
  32.5 1.7 %collective-permute-done.9.refs_1_.refs_6_ = bf16[1024,256]{1,0:T(8,128)(2,1)S(1)} collective-permute-done((bf16[1024,256]{1,0:T(8,128)(2,1)S(1)}, bf16[1024,256]{1,0:T(8,128)(2,1)S(1)}, u32[]{:S(2)}, u32[]{:S(2)}) %collective-permute-start.9) | collective-permute-done | bytes 524320 | tf_op jit(solution)/shard_map/ppermute | solution.py:326
  34.2 0.8 collective-permute-start.10
  35.0 2.0 %collective-permute-start.8 = (f32[80,256]{1,0:T(8,128)S(1)}, f32[80,256]{1,0:T(8,128)S(1)}, u32[]{:S(2)}, u32[]{:S(2)}) collective-permute-start(f32[80,256]{1,0:T(8,128)S(1)} %shard_map.70), channel_id=1, source_target_pairs={{0,12},{4,0},{8,4},{12,8},{1,13},{5,1},{9,5},{13,9},{2,14},{6,2},{... | collective-permute-start | bytes 245768 | tf_op jit(solution)/shard_map/ppermute | solution.py:337
  38.0 1.0 %collective-permute-done.8 = f32[80,256]{1,0:T(8,128)S(1)} collective-permute-done((f32[80,256]{1,0:T(8,128)S(1)}, f32[80,256]{1,0:T(8,128)S(1)}, u32[]{:S(2)}, u32[]{:S(2)}) %collective-permute-start.8) | collective-permute-done | bytes 81952 | tf_op jit(solution)/shard_map/ppermute | solution.py:337
  39.1 6.3 %collective-permute-done.7 = f32[80,256]{1,0:T(8,128)S(1)} collective-permute-done((f32[80,256]{1,0:T(8,128)S(1)}, f32[80,256]{1,0:T(8,128)S(1)}, u32[]{:S(2)}, u32[]{:S(2)}) %collective-permute-start.7) | collective-permute-done | bytes 81952 | tf_op jit(solution)/shard_map/ppermute | solution.py:337
  45.7 0.8 collective-permute-start.13
  46.6 2.4 %collective-permute-start.14 = (f32[128,256]{1,0:T(8,128)S(1)}, f32[128,256]{1,0:T(8,128)S(1)}, u32[]{:S(2)}, u32[]{:S(2)}) collective-permute-start(f32[128,256]{1,0:T(8,128)S(1)} %get-tuple-element.47), channel_id=1, source_target_pairs={{0,12},{4,0},{8,4},{12,8},{1,13},{5,1},{9,5},{13,9},{2,14},{6,2},{... | collective-permute-start | bytes 393224 | tf_op jit(solution)/shard_map/ppermute | solution.py:337
  49.0 2.1 %collective-permute-start.11 = (f32[4,80,256]{2,1,0:T(8,128)S(1)}, f32[4,80,256]{2,1,0:T(8,128)S(1)}, u32[]{:S(2)}, u32[]{:S(2)}) collective-permute-start(f32[4,80,256]{2,1,0:T(8,128)S(1)} %pad_maximum_fusion.1.refs_4_.refs_0_), channel_id=1, source_target_pairs={{0,1},{1,0},{2,3},{3,2},{4,5},{5,4},{6,7},{7,6},{8,9},{9,8},{10,11... | collective-permute-start | bytes 983048 | tf_op jit(solution)/shard_map/ppermute | solution.py:326
  51.1 0.8 collective-permute-done.12.refs_1_
  51.9 4.5 %collective-permute-done.13.refs_2_ = f32[128,256]{1,0:T(8,128)S(1)} collective-permute-done((f32[128,256]{1,0:T(8,128)S(1)}, f32[128,256]{1,0:T(8,128)S(1)}, u32[]{:S(2)}, u32[]{:S(2)}) %collective-permute-start.13) | collective-permute-done | bytes 131104 | tf_op jit(solution)/shard_map/ppermute | solution.py:337
  56.8 2.5 %collective-permute-start.19 = (f32[4,80,256]{2,1,0:T(8,128)S(1)}, f32[4,80,256]{2,1,0:T(8,128)S(1)}, u32[]{:S(2)}, u32[]{:S(2)}) collective-permute-start(f32[4,80,256]{2,1,0:T(8,128)S(1)} %collective-permute-done.18.refs_2_), channel_id=1, source_target_pairs={{0,1},{1,0},{2,3},{3,2},{4,5},{5,4},{6,7},{7,6},{8,9},{9,8},{10,11... | collective-permute-start | bytes 983048 | tf_op jit(solution)/shard_map/ppermute | solution.py:326
  59.3 3.0 %collective-permute-start.17 = (f32[128,256]{1,0:T(8,128)S(1)}, f32[128,256]{1,0:T(8,128)S(1)}, u32[]{:S(2)}, u32[]{:S(2)}) collective-permute-start(f32[128,256]{1,0:T(8,128)S(1)} %shard_map.72), channel_id=1, source_target_pairs={{0,12},{4,0},{8,4},{12,8},{1,13},{5,1},{9,5},{13,9},{2,14},{6,2},{... | collective-permute-start | bytes 393224 | tf_op jit(solution)/shard_map/ppermute | solution.py:337
  62.6 13.1 %shard_map.73 = (f32[512,512]{1,0:T(8,128)S(1)}, f32[1,512]{1,0:T(1,128)S(1)}) custom-call(f32[4,80,256]{2,1,0:T(8,128)S(1)} %pad_maximum_fusion.1.refs_4_.refs_0_, f32[4,80,256]{2,1,0:T(8,128)S(1)} %collective-permute-done.11.refs_1_, f32[4,80,256]{2,1,0:T(8,128)S(1)} %collective-permute-done.18.refs_2_, f32[4,80,256]{2,1,0:T(8,128)S(1)} %collective-permute-done.19.refs_3_), custom_call_target="tpu_custom_call" | custom-call | flops 16000000000 | bytes 4000000 | tf_op jit(solution)/shard_map/pallas_call | solution.py:315
  75.9 0.8 collective-permute-start.20
  76.6 1.5 %collective-permute-done.20.refs_3_ = f32[4,128,256]{2,1,0:T(8,128)S(1)} collective-permute-done((f32[4,128,256]{2,1,0:T(8,128)S(1)}, f32[4,128,256]{2,1,0:T(8,128)S(1)}, u32[]{:S(2)}, u32[]{:S(2)}) %collective-permute-start.20) | collective-permute-done | bytes 524320 | tf_op jit(solution)/shard_map/ppermute | solution.py:326
  78.2 19.0 %shard_map.74 = (f32[1024,256]{1,0:T(8,128)}, f32[1,256]{1,0:T(1,128)}) custom-call(f32[4,80,256]{2,1,0:T(8,128)S(1)} %pad_maximum_fusion.1.refs_4_.refs_0_, f32[4,80,256]{2,1,0:T(8,128)S(1)} %collective-permute-done.11.refs_1_, f32[4,128,256]{2,1,0:T(8,128)S(1)} %pad_maximum_fusion.refs_2_, f32[4,128,256]{2,1,0:T(8,128)S(1)} %collective-permute-done.20.refs_3_, ...), custom_call_target="tpu_custom_call" | custom-call | tf_op jit(solution)/shard_map/pallas_call | solution.py:315
  (28 shorter events, 3.6 us)
Async XLA Ops:
  0.6 1.2 %copy-start = (f32[2,4,128,256]{3,2,1,0:T(8,128)S(1)}, f32[2,4,128,256]{3,2,1,0:T(8,128)}, u32[]{:S(2)}) copy-start(f32[2,4,128,256]{3,2,1,0:T(8,128)} %tangent_ref.1) | copy-start | bytes 3145732
  1.9 0.7 copy-start.1
  2.5 0.7 copy-start.2
  3.2 0.7 copy-start.3
  5.0 7.4 %collective-permute-start = (bf16[11,32,256]{2,1,0:T(8,128)(2,1)S(1)}, bf16[11,32,256]{2,1,0:T(8,128)(2,1)S(1)}, u32[]{:S(2)}, u32[]{:S(2)}) collective-permute-start(bf16[11,32,256]{2,1,0:T(8,128)(2,1)S(1)} %get-tuple-element.31), channel_id=1, source_target_pairs={{0,4},{4,8},{8,12},{12,0},{1,5},{5,9},{9,13},{13,1},{2,6},{6,10},{... | collective-permute-start | bytes 540680 | tf_op jit(solution)/shard_map/ppermute | solution.py:635
  6.3 9.7 %collective-permute-start.1 = (bf16[11,32,256]{2,1,0:T(8,128)(2,1)S(1)}, bf16[11,32,256]{2,1,0:T(8,128)(2,1)S(1)}, u32[]{:S(2)}, u32[]{:S(2)}) collective-permute-start(bf16[11,32,256]{2,1,0:T(8,128)(2,1)S(1)} %get-tuple-element.32), channel_id=1, source_target_pairs={{4,0},{8,4},{12,8},{0,12},{5,1},{9,5},{13,9},{1,13},{6,2},{10,6},{... | collective-permute-start | bytes 540680 | tf_op jit(solution)/shard_map/ppermute | solution.py:635
  19.5 2.7 %collective-permute-start.2 = (bf16[1024,256]{1,0:T(8,128)(2,1)S(1)}, bf16[1024,256]{1,0:T(8,128)(2,1)S(1)}, u32[]{:S(2)}, u32[]{:S(2)}) collective-permute-start(bf16[1024,256]{1,0:T(8,128)(2,1)S(1)} %bitcast.11), channel_id=1, source_target_pairs={{0,1},{1,0},{2,3},{3,2},{4,5},{5,4},{6,7},{7,6},{8,9},{9,8},{10,11... | collective-permute-start | bytes 1572872 | tf_op jit(solution)/shard_map/ppermute | solution.py:326
  20.6 13.5 %collective-permute-start.9 = (bf16[1024,256]{1,0:T(8,128)(2,1)S(1)}, bf16[1024,256]{1,0:T(8,128)(2,1)S(1)}, u32[]{:S(2)}, u32[]{:S(2)}) collective-permute-start(bf16[1024,256]{1,0:T(8,128)(2,1)S(1)} %bitcast.12), channel_id=1, source_target_pairs={{0,2},{1,3},{2,0},{3,1},{4,6},{5,7},{6,4},{7,5},{8,10},{9,11},{10,... | collective-permute-start | bytes 1572872 | tf_op jit(solution)/shard_map/ppermute | solution.py:326
  22.8 5.6 %collective-permute-start.3 = (f32[80,256]{1,0:T(8,128)S(1)}, f32[80,256]{1,0:T(8,128)S(1)}, u32[]{:S(2)}, u32[]{:S(2)}) collective-permute-start(f32[80,256]{1,0:T(8,128)S(1)} %get-tuple-element.36), channel_id=1, source_target_pairs={{0,4},{4,8},{8,12},{12,0},{1,5},{5,9},{9,13},{13,1},{2,6},{6,10},{... | collective-permute-start | bytes 245768 | tf_op jit(solution)/shard_map/ppermute | solution.py:337
  23.7 8.7 %collective-permute-start.4 = (f32[80,256]{1,0:T(8,128)S(1)}, f32[80,256]{1,0:T(8,128)S(1)}, u32[]{:S(2)}, u32[]{:S(2)}) collective-permute-start(f32[80,256]{1,0:T(8,128)S(1)} %get-tuple-element.37), channel_id=1, source_target_pairs={{0,8},{4,12},{8,0},{12,4},{1,9},{5,13},{9,1},{13,5},{2,10},{6,14},... | collective-permute-start | bytes 245768 | tf_op jit(solution)/shard_map/ppermute | solution.py:337
  25.2 7.3 %collective-permute-start.5 = (f32[80,256]{1,0:T(8,128)S(1)}, f32[80,256]{1,0:T(8,128)S(1)}, u32[]{:S(2)}, u32[]{:S(2)}) collective-permute-start(f32[80,256]{1,0:T(8,128)S(1)} %get-tuple-element.38), channel_id=1, source_target_pairs={{0,12},{4,0},{8,4},{12,8},{1,13},{5,1},{9,5},{13,9},{2,14},{6,2},{... | collective-permute-start | bytes 245768 | tf_op jit(solution)/shard_map/ppermute | solution.py:337
  34.2 3.3 %collective-permute-start.10 = (bf16[1024,256]{1,0:T(8,128)(2,1)S(1)}, bf16[1024,256]{1,0:T(8,128)(2,1)S(1)}, u32[]{:S(2)}, u32[]{:S(2)}) collective-permute-start(bf16[1024,256]{1,0:T(8,128)(2,1)S(1)} %collective-permute-done.9.refs_1_.refs_6_), channel_id=1, source_target_pairs={{0,1},{1,0},{2,3},{3,2},{4,5},{5,4},{6,7},{7,6},{8,9},{9,8},{10,11... | collective-permute-start | bytes 1572872 | tf_op jit(solution)/shard_map/ppermute | solution.py:326
  35.0 4.1 %collective-permute-start.8 = (f32[80,256]{1,0:T(8,128)S(1)}, f32[80,256]{1,0:T(8,128)S(1)}, u32[]{:S(2)}, u32[]{:S(2)}) collective-permute-start(f32[80,256]{1,0:T(8,128)S(1)} %shard_map.70), channel_id=1, source_target_pairs={{0,12},{4,0},{8,4},{12,8},{1,13},{5,1},{9,5},{13,9},{2,14},{6,2},{... | collective-permute-start | bytes 245768 | tf_op jit(solution)/shard_map/ppermute | solution.py:337
  37.0 8.4 %collective-permute-start.7 = (f32[80,256]{1,0:T(8,128)S(1)}, f32[80,256]{1,0:T(8,128)S(1)}, u32[]{:S(2)}, u32[]{:S(2)}) collective-permute-start(f32[80,256]{1,0:T(8,128)S(1)} %shard_map.70), channel_id=1, source_target_pairs={{0,8},{4,12},{8,0},{12,4},{1,9},{5,13},{9,1},{13,5},{2,10},{6,14},... | collective-permute-start | bytes 245768 | tf_op jit(solution)/shard_map/ppermute | solution.py:337
  37.0 8.4 %collective-permute-start.6 = (f32[80,256]{1,0:T(8,128)S(1)}, f32[80,256]{1,0:T(8,128)S(1)}, u32[]{:S(2)}, u32[]{:S(2)}) collective-permute-start(f32[80,256]{1,0:T(8,128)S(1)} %shard_map.70), channel_id=1, source_target_pairs={{0,4},{4,8},{8,12},{12,0},{1,5},{5,9},{9,13},{13,1},{2,6},{6,10},{... | collective-permute-start | bytes 245768 | tf_op jit(solution)/shard_map/ppermute | solution.py:337
  45.4 11.4 %collective-permute-start.18 = (f32[4,80,256]{2,1,0:T(8,128)S(1)}, f32[4,80,256]{2,1,0:T(8,128)S(1)}, u32[]{:S(2)}, u32[]{:S(2)}) collective-permute-start(f32[4,80,256]{2,1,0:T(8,128)S(1)} %pad_maximum_fusion.1.refs_4_.refs_0_), channel_id=1, source_target_pairs={{0,2},{1,3},{2,0},{3,1},{4,6},{5,7},{6,4},{7,5},{8,10},{9,11},{10,... | collective-permute-start | bytes 983048 | tf_op jit(solution)/shard_map/ppermute | solution.py:326
  45.7 6.2 %collective-permute-start.12 = (f32[128,256]{1,0:T(8,128)S(1)}, f32[128,256]{1,0:T(8,128)S(1)}, u32[]{:S(2)}, u32[]{:S(2)}) collective-permute-start(f32[128,256]{1,0:T(8,128)S(1)} %get-tuple-element.45), channel_id=1, source_target_pairs={{0,4},{4,8},{8,12},{12,0},{1,5},{5,9},{9,13},{13,1},{2,6},{6,10},{... | collective-permute-start | bytes 393224 | tf_op jit(solution)/shard_map/ppermute | solution.py:337
  45.7 10.7 %collective-permute-start.13 = (f32[128,256]{1,0:T(8,128)S(1)}, f32[128,256]{1,0:T(8,128)S(1)}, u32[]{:S(2)}, u32[]{:S(2)}) collective-permute-start(f32[128,256]{1,0:T(8,128)S(1)} %get-tuple-element.46), channel_id=1, source_target_pairs={{0,8},{4,12},{8,0},{12,4},{1,9},{5,13},{9,1},{13,5},{2,10},{6,14},... | collective-permute-start | bytes 393224 | tf_op jit(solution)/shard_map/ppermute | solution.py:337
  46.6 10.2 %collective-permute-start.14 = (f32[128,256]{1,0:T(8,128)S(1)}, f32[128,256]{1,0:T(8,128)S(1)}, u32[]{:S(2)}, u32[]{:S(2)}) collective-permute-start(f32[128,256]{1,0:T(8,128)S(1)} %get-tuple-element.47), channel_id=1, source_target_pairs={{0,12},{4,0},{8,4},{12,8},{1,13},{5,1},{9,5},{13,9},{2,14},{6,2},{... | collective-permute-start | bytes 393224 | tf_op jit(solution)/shard_map/ppermute | solution.py:337
  49.0 13.6 %collective-permute-start.11 = (f32[4,80,256]{2,1,0:T(8,128)S(1)}, f32[4,80,256]{2,1,0:T(8,128)S(1)}, u32[]{:S(2)}, u32[]{:S(2)}) collective-permute-start(f32[4,80,256]{2,1,0:T(8,128)S(1)} %pad_maximum_fusion.1.refs_4_.refs_0_), channel_id=1, source_target_pairs={{0,1},{1,0},{2,3},{3,2},{4,5},{5,4},{6,7},{7,6},{8,9},{9,8},{10,11... | collective-permute-start | bytes 983048 | tf_op jit(solution)/shard_map/ppermute | solution.py:326
  56.8 5.9 %collective-permute-start.19 = (f32[4,80,256]{2,1,0:T(8,128)S(1)}, f32[4,80,256]{2,1,0:T(8,128)S(1)}, u32[]{:S(2)}, u32[]{:S(2)}) collective-permute-start(f32[4,80,256]{2,1,0:T(8,128)S(1)} %collective-permute-done.18.refs_2_), channel_id=1, source_target_pairs={{0,1},{1,0},{2,3},{3,2},{4,5},{5,4},{6,7},{7,6},{8,9},{9,8},{10,11... | collective-permute-start | bytes 983048 | tf_op jit(solution)/shard_map/ppermute | solution.py:326
  59.3 16.5 %collective-permute-start.17 = (f32[128,256]{1,0:T(8,128)S(1)}, f32[128,256]{1,0:T(8,128)S(1)}, u32[]{:S(2)}, u32[]{:S(2)}) collective-permute-start(f32[128,256]{1,0:T(8,128)S(1)} %shard_map.72), channel_id=1, source_target_pairs={{0,12},{4,0},{8,4},{12,8},{1,13},{5,1},{9,5},{13,9},{2,14},{6,2},{... | collective-permute-start | bytes 393224 | tf_op jit(solution)/shard_map/ppermute | solution.py:337
  62.3 13.5 %collective-permute-start.16 = (f32[128,256]{1,0:T(8,128)S(1)}, f32[128,256]{1,0:T(8,128)S(1)}, u32[]{:S(2)}, u32[]{:S(2)}) collective-permute-start(f32[128,256]{1,0:T(8,128)S(1)} %shard_map.72), channel_id=1, source_target_pairs={{0,8},{4,12},{8,0},{12,4},{1,9},{5,13},{9,1},{13,5},{2,10},{6,14},... | collective-permute-start | bytes 393224 | tf_op jit(solution)/shard_map/ppermute | solution.py:337
  62.5 13.3 %collective-permute-start.15 = (f32[128,256]{1,0:T(8,128)S(1)}, f32[128,256]{1,0:T(8,128)S(1)}, u32[]{:S(2)}, u32[]{:S(2)}) collective-permute-start(f32[128,256]{1,0:T(8,128)S(1)} %shard_map.72), channel_id=1, source_target_pairs={{0,4},{4,8},{8,12},{12,0},{1,5},{5,9},{9,13},{13,1},{2,6},{6,10},{... | collective-permute-start | bytes 393224 | tf_op jit(solution)/shard_map/ppermute | solution.py:337
  75.9 2.3 %collective-permute-start.20 = (f32[4,128,256]{2,1,0:T(8,128)S(1)}, f32[4,128,256]{2,1,0:T(8,128)S(1)}, u32[]{:S(2)}, u32[]{:S(2)}) collective-permute-start(f32[4,128,256]{2,1,0:T(8,128)S(1)} %pad_maximum_fusion.refs_2_), channel_id=1, source_target_pairs={{0,1},{1,0},{2,3},{3,2},{4,5},{5,4},{6,7},{7,6},{8,9},{9,8},{10,11... | collective-permute-start | bytes 1572872 | tf_op jit(solution)/shard_map/ppermute | solution.py:326
